TPU v7x, 128 devices: a whole 4x4x4 slice. The times are simulated.
128 devices in a mesh: dp: 8 (over z, core), expert: 16 (over y, x).
Axes of the slice: x: 4, y: 4, z: 4, core: 2. Of those that a mesh axis runs over, the one named last changes fastest.
Arguments:
- tokens: bfloat16 [16384, 2048], P(('dp', 'expert')), may hold values from -24 to 24
- expert_ids: int32 [16384, 6], P(('dp', 'expert')), may hold values from 0 to 31, all different within a row; in each aligned block of 128 rows (0 to 127, 128 to 255, ...) at most 32 rows name the same one
- combine_weight: float32 [16384, 6], P(('dp', 'expert')), may hold values from 0.05 to 1
- partner: int32 [16], replicated, may hold values from 0 to 15, as said below
- w_up: bfloat16 [2048, 32, 768], P(None, 'expert'), may hold values from -0.125 to 0.125
- w_down: bfloat16 [2048, 32, 768], P(None, 'expert'), may hold values from -0.21875 to 0.21875
- out_grad: bfloat16 [16384, 2048], P(('dp', 'expert')), may hold values from -6 to 6
Outputs:
- output: bfloat16 [16384, 2048], P(('dp', 'expert'))
- input_grad: bfloat16 [16384, 2048], P(('dp', 'expert'))
- grad_up: bfloat16 [2048, 32, 768], P('dp', 'expert')
- grad_down: bfloat16 [2048, 32, 768], P('dp', 'expert')
Inputs may be any that keep to these rules, and one draw needn't show every extreme that they name: `expert_ids`: each token names 6 different experts; among the tokens of one device (aligned blocks of 128 tokens) no expert is named more than 32 times, and in some blocks one is named exactly 32 times. partner[partner[j]] = j and partner[j] != j for every j.
All inputs are finite; a program needn't handle non-finite values.
Results may differ from a plain program's by a relative error of at most 0.017.
Values may be sent and summed in bfloat16 or wider, within the bound.
A program may use at most 192 MiB of HBM per device.

v0:
```python
import jax
import jax.numpy as jnp
from jax import lax
from jax.sharding import PartitionSpec as P


def silu_slope(hidden_pre):
    sigma = jax.nn.sigmoid(hidden_pre)
    return sigma * (1.0 + hidden_pre * (1.0 - sigma))


def body(tokens, expert_ids, combine_weight, partner, w_up, w_down, out_grad):
    owners = lax.axis_size("expert")
    tok_dev, chosen = expert_ids.shape
    model_width = tokens.shape[1]
    local_slots = w_up.shape[1]
    hidden = w_up.shape[2]
    experts = local_slots * owners
    capacity = max(2, tok_dev * chosen * 4 // (3 * experts))
    assigns = tok_dev * chosen
    named = expert_ids.reshape(assigns)
    onehot = (named[:, None] == jnp.arange(experts, dtype=jnp.int32)[None, :]).astype(jnp.int32)
    earlier = jnp.cumsum(onehot, axis=0) - onehot
    position = jnp.sum(earlier * onehot, axis=1)
    anchor_dev = named // local_slots
    local_slot = named % local_slots
    holder = jnp.where(local_slot == 0, partner[anchor_dev], anchor_dev)
    up_first = w_up[:, 0, :].reshape(owners, model_width // owners, hidden)
    down_first = w_down[:, 0, :].reshape(owners, model_width // owners, hidden)
    spread = (
        lax.all_to_all(up_first, "expert", split_axis=0, concat_axis=0, tiled=True),
        lax.all_to_all(down_first, "expert", split_axis=0, concat_axis=0, tiled=True),
    )
    picked = (spread[0][partner], spread[1][partner])
    moved = (
        lax.all_to_all(picked[0], "expert", split_axis=0, concat_axis=0, tiled=True),
        lax.all_to_all(picked[1], "expert", split_axis=0, concat_axis=0, tiled=True),
    )
    up_mats = [moved[0].reshape(model_width, hidden)]
    down_mats = [moved[1].reshape(model_width, hidden)]
    slot_index = 1
    up_mats.append(w_up[:, slot_index, :])
    down_mats.append(w_down[:, slot_index, :])
    flat_slot = (holder * local_slots + local_slot) * capacity + position
    assign_src = jnp.full((owners * local_slots * capacity,), assigns, jnp.int32)
    assign_src = assign_src.at[flat_slot].set(jnp.arange(assigns, dtype=jnp.int32))
    source = assign_src // chosen
    padded_tokens = jnp.concatenate([tokens, jnp.zeros((1, model_width), tokens.dtype)], axis=0)
    outgoing = padded_tokens[source].reshape(owners, local_slots, capacity, model_width)
    incoming = lax.all_to_all(outgoing, "expert", split_axis=0, concat_axis=0, tiled=True)
    slot_rows = owners * capacity
    inputs_all = []
    hidden_all = []
    activ_all = []
    outputs_all = []
    for slot_index in range(local_slots):
        inputs = incoming[:, slot_index].reshape(slot_rows, model_width)
        hidden_pre = jnp.dot(inputs, up_mats[slot_index], preferred_element_type=jnp.float32)
        activated = jax.nn.silu(hidden_pre).astype(jnp.bfloat16)
        expert_out = lax.dot_general(
            activated,
            down_mats[slot_index],
            (((1,), (1,)), ((), ())),
            preferred_element_type=jnp.float32,
        ).astype(jnp.bfloat16)
        inputs_all.append(inputs)
        hidden_all.append(hidden_pre)
        activ_all.append(activated)
        outputs_all.append(expert_out.reshape(owners, capacity, model_width))
    out_buffer = jnp.stack(outputs_all, axis=1)
    returned = lax.all_to_all(
        out_buffer, "expert", split_axis=0, concat_axis=0, tiled=True
    ).reshape(-1, model_width)
    gathered = returned[flat_slot].reshape(tok_dev, chosen, model_width).astype(jnp.float32)
    output = jnp.sum(combine_weight[:, :, None] * gathered, axis=1).astype(jnp.bfloat16)
    grad_rows = (combine_weight[:, :, None] * out_grad[:, None, :].astype(jnp.float32)).astype(
        jnp.bfloat16
    )
    grad_rows = jnp.concatenate(
        [grad_rows.reshape(assigns, model_width), jnp.zeros((1, model_width), jnp.bfloat16)], axis=0
    )
    grad_send = grad_rows[assign_src].reshape(owners, local_slots, capacity, model_width)
    grad_arrived = lax.all_to_all(grad_send, "expert", split_axis=0, concat_axis=0, tiled=True)
    gradout_all = []
    gradpre_all = []
    gradin_all = []
    for slot_index in range(local_slots):
        grad_out = grad_arrived[:, slot_index].reshape(slot_rows, model_width)
        grad_act = jnp.dot(grad_out, down_mats[slot_index], preferred_element_type=jnp.float32)
        grad_pre = (grad_act * silu_slope(hidden_all[slot_index])).astype(jnp.bfloat16)
        grad_in = lax.dot_general(
            grad_pre,
            up_mats[slot_index],
            (((1,), (1,)), ((), ())),
            preferred_element_type=jnp.float32,
        ).astype(jnp.bfloat16)
        gradout_all.append(grad_out)
        gradpre_all.append(grad_pre)
        gradin_all.append(grad_in.reshape(owners, capacity, model_width))
    grad_buffer = jnp.stack(gradin_all, axis=1)
    grad_back = lax.all_to_all(
        grad_buffer, "expert", split_axis=0, concat_axis=0, tiled=True
    ).reshape(-1, model_width)
    grad_gathered = grad_back[flat_slot].reshape(tok_dev, chosen, model_width).astype(jnp.float32)
    input_grad = jnp.sum(grad_gathered, axis=1).astype(jnp.bfloat16)
    grad_scale = 1.0 / tok_dev
    up_terms = []
    down_terms = []
    for slot_index in range(local_slots):
        input_cols = inputs_all[slot_index]
        outg_cols = gradout_all[slot_index]
        up_terms.append(
            lax.dot_general(
                input_cols,
                gradpre_all[slot_index],
                (((0,), (0,)), ((), ())),
                preferred_element_type=jnp.float32,
            )
        )
        down_terms.append(
            lax.dot_general(
                outg_cols,
                activ_all[slot_index],
                (((0,), (0,)), ((), ())),
                preferred_element_type=jnp.float32,
            )
        )
    summed = lax.psum_scatter(
        (
            jnp.stack([jnp.stack(up_terms, axis=1), jnp.stack(down_terms, axis=1)], axis=1)
            * grad_scale
        ).astype(jnp.bfloat16),
        "dp",
        scatter_dimension=0,
        tiled=True,
    ).astype(jnp.float32)
    grad_up = summed[:, 0].astype(jnp.bfloat16)
    grad_down = summed[:, 1].astype(jnp.bfloat16)
    return (output, input_grad, grad_up, grad_down)


def solution(mesh):
    return jax.shard_map(
        body,
        mesh=mesh,
        in_specs=(
            P(("dp", "expert"), None),
            P(("dp", "expert"), None),
            P(("dp", "expert"), None),
            P(),
            P(None, "expert", None),
            P(None, "expert", None),
            P(("dp", "expert"), None),
        ),
        out_specs=(
            P(("dp", "expert"), None),
            P(("dp", "expert"), None),
            P("dp", "expert", None),
            P("dp", "expert", None),
        ),
        check_vma=False,
    )
```

profile of v0, /device:TPU:0, one launch (start us, length us, event | category | flops | bytes accessed | tf_op | source)
XLA Modules:
  0.0 560.4 jit_solution(3145677214393858817)
XLA Ops:
  7.2 13.5 %fusion.16 = (bf16[2048,1,768]{2,1,0:T(2,128)(2,1)S(1)}, bf16[2048,1,768]{2,1,0:T(2,128)(2,1)}) fusion(bf16[2048,2,768]{2,1,0:T(2,128)(2,1)} %param.12), kind=kLoop, calls=%fused_computation.85 | loop fusion | bytes 12582912 | tf_op jit(solution)/shard_map/slice | solution.py:29
  22.8 7.1 %all-to-all-start.3 = ((bf16[16,128,768]{2,1,0:T(8,128)(2,1)}), bf16[16,128,768]{2,1,0:T(8,128)(2,1)S(1)}, u32[]{:S(2)}, u32[]{:S(2)}) async-start(bf16[16,128,768]{2,1,0:T(8,128)(2,1)} %bitcast.103), calls=%async_computation.3 | async-start | bytes 6291456 | tf_op jit(solution)/shard_map/all_to_all | solution.py:32
  29.9 13.6 %fusion.15 = (bf16[2048,1,768]{2,1,0:T(2,128)(2,1)S(1)}, bf16[2048,1,768]{2,1,0:T(2,128)(2,1)}) fusion(bf16[2048,2,768]{2,1,0:T(2,128)(2,1)} %param.11), kind=kLoop, calls=%fused_computation.84 | loop fusion | bytes 12582912 | tf_op jit(solution)/shard_map/slice | solution.py:28
  45.7 31.7 %all-to-all-done.3 = bf16[16,128,768]{2,1,0:T(8,128)(2,1)S(1)} async-done(((bf16[16,128,768]{2,1,0:T(8,128)(2,1)}), bf16[16,128,768]{2,1,0:T(8,128)(2,1)S(1)}, u32[]{:S(2)}, u32[]{:S(2)}) %all-to-all-start.3) | async-done | bytes 3145760 | tf_op jit(solution)/shard_map/all_to_all | solution.py:32
  92.7 5.6 %select_select_fusion = s32[768]{0:T(1024)S(1)} fusion(pred[768]{0:T(1024)(128)(4,1)S(1)} %get-tuple-element.24, pred[768]{0:T(1024)(128)(4,1)S(1)} %get-tuple-element.23, pred[768]{0:T(1024)(128)(4,1)S(1)} %get-tuple-element.22, pred[768]{0:T(1024)(128)(4,1)S(1)} %get-tuple-element.21, pred[768]{0:T(1024)(128)(4,1)S(1)} %get-tuple-element.20, ...), kind=kLoop, calls=%fused_computation.73 | loop fusion | flops 6912 | bytes 13092 | tf_op jit(solution)/shard_map/gather | solution.py:27
  101.8 6.0 %gather_fusion = bf16[1024,2048]{1,0:T(8,128)(2,1)} fusion(bf16[129,2048]{1,0:T(8,128)(2,1)S(1)} %concatenate.6, s32[1024]{0:T(1024)S(1)} %get-tuple-element.39), kind=kCustom, calls=%fused_computation | custom fusion | bytes 8392704 | tf_op jit(solution)/shard_map/gather | solution.py:49
  107.9 20.7 %all-to-all-done.1 = bf16[16,128,768]{2,1,0:T(8,128)(2,1)} async-done(((bf16[16,128,768]{2,1,0:T(8,128)(2,1)}), bf16[16,128,768]{2,1,0:T(8,128)(2,1)}, u32[]{:S(2)}, u32[]{:S(2)}) %all-to-all-start.1) | async-done | bytes 3145760 | tf_op jit(solution)/shard_map/all_to_all | solution.py:31
  128.5 4.7 all-to-all-start
  137.6 8.3 %mul.95 = f32[768,2048]{1,0:T(8,128)} reshape(f32[128,6,2048]{2,1,0:T(8,128)} %mul.94) | data formatting | bytes 12582912 | tf_op jit(solution)/shard_map/mul | solution.py:76
  149.4 6.0 %gather_fusion.4 = bf16[1024,2048]{1,0:T(8,128)(2,1)} fusion(bf16[769,2048]{1,0:T(8,128)(2,1)S(1)} %concatenate.7, s32[1024]{0:T(1024)S(1)} %get-tuple-element.38), kind=kCustom, calls=%fused_computation.4 | custom fusion | bytes 8392704 | tf_op jit(solution)/shard_map/gather | solution.py:82
  155.5 34.8 %all-to-all-done = bf16[16,2,32,2048]{3,2,1,0:T(8,128)(2,1)} async-done(((bf16[16,2,32,2048]{3,2,1,0:T(8,128)(2,1)}), bf16[16,2,32,2048]{3,2,1,0:T(8,128)(2,1)}, u32[]{:S(2)}, u32[]{:S(2)}) %all-to-all-start) | async-done | bytes 4194336 | tf_op jit(solution)/shard_map/all_to_all | solution.py:50
  199.3 51.0 %all-to-all-done.6 = bf16[16,2,32,2048]{3,2,1,0:T(8,128)(2,1)} async-done(((bf16[16,2,32,2048]{3,2,1,0:T(8,128)(2,1)}), bf16[16,2,32,2048]{3,2,1,0:T(8,128)(2,1)}, u32[]{:S(2)}, u32[]{:S(2)}) %all-to-all-start.6) | async-done | bytes 4194336 | tf_op jit(solution)/shard_map/all_to_all | solution.py:83
  257.2 4.8 fusion.18
  262.0 4.8 fusion.17
  266.8 29.8 %all-to-all-done.2 = bf16[16,128,768]{2,1,0:T(8,128)(2,1)} async-done(((bf16[16,128,768]{2,1,0:T(8,128)(2,1)}), bf16[16,128,768]{2,1,0:T(8,128)(2,1)}, u32[]{:S(2)}, u32[]{:S(2)}) %all-to-all-start.2) | async-done | bytes 3145760 | tf_op jit(solution)/shard_map/all_to_all | solution.py:36
  301.5 5.4 fusion.1
  328.6 16.6 %all-to-all-done.4 = bf16[16,128,768]{2,1,0:T(8,128)(2,1)} async-done(((bf16[16,128,768]{2,1,0:T(8,128)(2,1)}), bf16[16,128,768]{2,1,0:T(8,128)(2,1)}, u32[]{:S(2)}, u32[]{:S(2)}) %all-to-all-start.4) | async-done | bytes 3145760 | tf_op jit(solution)/shard_map/all_to_all | solution.py:37
  345.2 4.9 multiply_convert_fusion.2
  351.1 4.8 convolution_bitcast_fusion.3
  355.9 10.0 %maximum_bitcast_fusion.1 = f32[2048,1,2,768]{3,0,2,1:T(8,128)} fusion(f32[2048,1,768]{2,0,1:T(8,128)} %convolution_bitcast_fusion, f32[2048,1,768]{2,0,1:T(8,128)} %convolution_bitcast_fusion.1), kind=kLoop, calls=%fused_computation.10 | loop fusion | flops 3145728 | bytes 25165824 | tf_op jit(solution)/shard_map/stack | solution.py:130
  365.9 8.8 %maximum_bitcast_fusion = f32[2048,1,2,768]{3,0,2,1:T(8,128)} fusion(f32[2048,1,768]{2,0,1:T(8,128)S(1)} %bitcast.107, f32[2048,1,768]{2,0,1:T(8,128)} %convolution_bitcast_fusion.3), kind=kLoop, calls=%fused_computation.9 | loop fusion | flops 3145728 | bytes 25165824 | tf_op jit(solution)/shard_map/stack | solution.py:130
  374.8 13.7 %fusion = bf16[2048,2,2,768]{3,0,2,1:T(8,128)(2,1)} fusion(f32[2048,1,2,768]{3,0,2,1:T(8,128)} %maximum_bitcast_fusion.1, f32[2048,1,2,768]{3,0,2,1:T(8,128)} %maximum_bitcast_fusion), kind=kLoop, calls=%fused_computation.8 | loop fusion | flops 18874368 | bytes 37748736 | tf_op jit(solution)/shard_map/convert_element_type | solution.py:132
  389.9 4.7 convolution_convert_fusion.2
  401.0 4.7 all-to-all-start.5
  405.7 4.8 convolution_convert_fusion
  416.8 45.8 %all-to-all-done.5 = bf16[16,2,32,2048]{3,2,1,0:T(8,128)(2,1)} async-done(((bf16[16,2,32,2048]{3,2,1,0:T(8,128)(2,1)}), bf16[16,2,32,2048]{3,2,1,0:T(8,128)(2,1)}, u32[]{:S(2)}, u32[]{:S(2)}) %all-to-all-start.5) | async-done | bytes 4194336 | tf_op jit(solution)/shard_map/all_to_all | solution.py:71
  462.6 4.7 all-to-all-start.7
  467.3 9.1 %gather_fusion.3 = bf16[768,2048]{1,0:T(8,128)(2,1)S(1)} fusion(bf16[1024,2048]{1,0:T(8,128)(2,1)} %bitcast.30, s32[1024]{0:T(1024)S(1)} %pad_clamp_fusion), kind=kCustom, calls=%fused_computation.3 | custom fusion | bytes 6294528 | tf_op jit(solution)/shard_map/gather | solution.py:74
  480.1 43.4 %all-to-all-done.7 = bf16[16,2,32,2048]{3,2,1,0:T(8,128)(2,1)} async-done(((bf16[16,2,32,2048]{3,2,1,0:T(8,128)(2,1)}), bf16[16,2,32,2048]{3,2,1,0:T(8,128)(2,1)}, u32[]{:S(2)}, u32[]{:S(2)}) %all-to-all-start.7) | async-done | bytes 4194336 | tf_op jit(solution)/shard_map/all_to_all | solution.py:101
  523.5 9.1 %gather_fusion.5 = bf16[768,2048]{1,0:T(8,128)(2,1)S(1)} fusion(bf16[1024,2048]{1,0:T(8,128)(2,1)} %bitcast.38, s32[1024]{0:T(1024)S(1)} %pad_clamp_fusion), kind=kCustom, calls=%fused_computation.5 | custom fusion | bytes 6294528 | tf_op jit(solution)/shard_map/gather | solution.py:104
  535.5 5.7 %reduce_sum.35 = bf16[128,2048]{1,0:T(8,128)(2,1)} reduce(bf16[128,6,2048]{2,1,0:T(8,128)(2,1)} %reshape.220, bf16[]{:T(256)} %constant.34.clone.1), dimensions={1}, to_apply=%region_5.6 | reduce | flops 1310720 | bytes 3670018 | tf_op jit(solution)/shard_map/reduce_sum | solution.py:105
  541.1 7.4 %multiply_reduce_fusion = bf16[128,2048]{1,0:T(8,128)(2,1)} fusion(f32[128,6,2048]{2,1,0:T(8,128)} %reshape.221, f32[128,6]{1,0:T(8,128)S(1)} %copy.30), kind=kLoop, calls=%fused_computation.11 | loop fusion | flops 2883584 | bytes 6818816 | tf_op jit(solution)/shard_map/reduce_sum | solution.py:75
  (96 shorter events, 99.5 us)
Async XLA Ops:
  22.8 54.6 %all-to-all-start.3 = ((bf16[16,128,768]{2,1,0:T(8,128)(2,1)}), bf16[16,128,768]{2,1,0:T(8,128)(2,1)S(1)}, u32[]{:S(2)}, u32[]{:S(2)}) async-start(bf16[16,128,768]{2,1,0:T(8,128)(2,1)} %bitcast.103), calls=%async_computation.3 | async-start | bytes 6291456 | tf_op jit(solution)/shard_map/all_to_all | solution.py:32
  77.4 1.7 copy-start
  77.4 6.2 %copy-start.8 = (s32[128,6]{0,1:T(8,128)S(1)}, s32[128,6]{0,1:T(8,128)}, u32[]{:S(2)}) copy-start(s32[128,6]{0,1:T(8,128)} %param.8) | copy-start | bytes 9220
  77.4 9.9 %copy-start.7 = (s32[16]{0:T(128)S(1)}, s32[16]{0:T(128)}, u32[]{:S(2)}) copy-start(s32[16]{0:T(128)} %param.10) | copy-start | bytes 196
  79.1 49.4 %all-to-all-start.1 = ((bf16[16,128,768]{2,1,0:T(8,128)(2,1)}), bf16[16,128,768]{2,1,0:T(8,128)(2,1)}, u32[]{:S(2)}, u32[]{:S(2)}) async-start(bf16[16,128,768]{2,1,0:T(8,128)(2,1)} %bitcast.102), calls=%async_computation.1 | async-start | bytes 6291456 | tf_op jit(solution)/shard_map/all_to_all | solution.py:31
  128.5 4.7 copy-start.9
  128.5 4.8 copy-start.6
  128.5 61.8 %all-to-all-start = ((bf16[16,2,32,2048]{3,2,1,0:T(8,128)(2,1)}), bf16[16,2,32,2048]{3,2,1,0:T(8,128)(2,1)}, u32[]{:S(2)}, u32[]{:S(2)}) async-start(bf16[16,2,32,2048]{3,2,1,0:T(8,128)(2,1)} %bitcast.100), calls=%async_computation | async-start | bytes 8388608 | tf_op jit(solution)/shard_map/all_to_all | solution.py:50
  190.3 60.0 %all-to-all-start.6 = ((bf16[16,2,32,2048]{3,2,1,0:T(8,128)(2,1)}), bf16[16,2,32,2048]{3,2,1,0:T(8,128)(2,1)}, u32[]{:S(2)}, u32[]{:S(2)}) async-start(bf16[16,2,32,2048]{3,2,1,0:T(8,128)(2,1)} %bitcast.101), calls=%async_computation.6 | async-start | bytes 8388608 | tf_op jit(solution)/shard_map/all_to_all | solution.py:83
  199.3 55.5 %copy-start.1 = (bf16[16,128,768]{2,1,0:T(8,128)(2,1)S(1)}, bf16[16,128,768]{2,1,0:T(8,128)(2,1)}, u32[]{:S(2)}) copy-start(bf16[16,128,768]{2,1,0:T(8,128)(2,1)} %copy-done) | copy-start | bytes 9437188
  250.3 46.4 %all-to-all-start.2 = ((bf16[16,128,768]{2,1,0:T(8,128)(2,1)}), bf16[16,128,768]{2,1,0:T(8,128)(2,1)}, u32[]{:S(2)}, u32[]{:S(2)}) async-start(bf16[16,128,768]{2,1,0:T(8,128)(2,1)} %gather_fusion.1), calls=%async_computation.2 | async-start | bytes 6291456 | tf_op jit(solution)/shard_map/all_to_all | solution.py:36
  296.6 10.2 %slice-start = ((s8[6291456]{0:T(1024)(128)(4,1)}), s8[2097152]{0:T(1024)(128)(4,1)S(1)}, s32[]{:S(2)}) async-start(s8[6291456]{0:T(1024)(128)(4,1)} %bitcast.104), calls=%async_computation.10 | async-start | bytes 4194304
  296.6 48.6 %all-to-all-start.4 = ((bf16[16,128,768]{2,1,0:T(8,128)(2,1)}), bf16[16,128,768]{2,1,0:T(8,128)(2,1)}, u32[]{:S(2)}, u32[]{:S(2)}) async-start(bf16[16,128,768]{2,1,0:T(8,128)(2,1)} %gather_fusion.2), calls=%async_computation.4 | async-start | bytes 6291456 | tf_op jit(solution)/shard_map/all_to_all | solution.py:37
  301.3 247.3 %reduce-scatter.2.cloned.1.call-start = ((), (), s32[]{:S(2)}) async-start(), calls=%async_computation.9 | async-start | bytes 14155776 | tf_op jit(solution)/shard_map/reduce_scatter | solution.py:128
  301.5 5.4 slice-start.1
  301.5 5.4 copy-start.5
  306.9 7.5 %copy-start.14 = (f32[512,768]{1,0:T(8,128)}, f32[512,768]{1,0:T(8,128)S(1)}, u32[]{:S(2)}) copy-start(f32[512,768]{1,0:T(8,128)S(1)} %fusion.1) | copy-start | bytes 4718596
  306.9 2.9 copy-start.4
  309.0 0.9 copy-start.10
  314.3 4.6 copy-start.2
  318.9 5.0 copy-start.3
  322.8 1.2 copy-start.16
  350.2 0.9 copy-start.12
  351.1 14.9 %slice-start.2 = ((s8[6291456]{0:T(1024)(128)(4,1)}), s8[4194304]{0:T(1024)(128)(4,1)S(1)}, s32[]{:S(2)}) async-start(s8[6291456]{0:T(1024)(128)(4,1)} %bitcast.106), calls=%async_computation.12 | async-start | bytes 8388608
  355.9 10.0 %slice-start.3 = ((s8[6291456]{0:T(1024)(128)(4,1)}), s8[2097152]{0:T(1024)(128)(4,1)S(1)}, s32[]{:S(2)}) async-start(s8[6291456]{0:T(1024)(128)(4,1)} %bitcast.106), calls=%async_computation.13 | async-start | bytes 4194304
  388.5 1.4 copy-start.15
  389.9 4.8 copy-start.17
  401.0 4.7 copy-start.11
  401.0 61.6 %all-to-all-start.5 = ((bf16[16,2,32,2048]{3,2,1,0:T(8,128)(2,1)}), bf16[16,2,32,2048]{3,2,1,0:T(8,128)(2,1)}, u32[]{:S(2)}, u32[]{:S(2)}) async-start(bf16[16,2,32,2048]{3,2,1,0:T(8,128)(2,1)} %pad_maximum_fusion), calls=%async_computation.5 | async-start | bytes 8388608 | tf_op jit(solution)/shard_map/all_to_all | solution.py:71
  405.7 4.8 copy-start.13
  462.6 60.9 %all-to-all-start.7 = ((bf16[16,2,32,2048]{3,2,1,0:T(8,128)(2,1)}), bf16[16,2,32,2048]{3,2,1,0:T(8,128)(2,1)}, u32[]{:S(2)}, u32[]{:S(2)}) async-start(bf16[16,2,32,2048]{3,2,1,0:T(8,128)(2,1)} %pad_maximum_fusion.1), calls=%async_computation.7 | async-start | bytes 8388608 | tf_op jit(solution)/shard_map/all_to_all | solution.py:101
Sparse Core Ops, SparseCore 0:
  388.7 71.4 reduce-scatter.1
where the time goes:
time: 570 us; the launch traced here: 560 us
  waiting for transfers between devices  274 us (48%)
  local copies, waits for them, and re-layouts  114 us (20%)
  other arithmetic  65.6 us (12%)
  matrix products  52.2 us (9%)
  starting transfers between devices  39.5 us (7%)
  between operations  14.7 us (3%)
    all_to_all x1, waiting for transfers between devices, body(): lax.all_to_all(grad_send, 'expert', split_axis=0, concat_axis=0, tiled=True)  51 us
    all_to_all x1, waiting for transfers between devices, body(): lax.all_to_all(out_buffer, 'expert', split_axis=0, concat_axis=0, tiled=T...  45.8 us
    all_to_all x1, waiting for transfers between devices, body(): lax.all_to_all(grad_buffer, 'expert', split_axis=0, concat_axis=0, tiled=...  43.4 us
    all_to_all x1, waiting for transfers between devices, body(): lax.all_to_all(outgoing, 'expert', split_axis=0, concat_axis=0, tiled=True)  34.8 us
    all_to_all x1, waiting for transfers between devices, body(): lax.all_to_all(down_first, 'expert', split_axis=0, concat_axis=0, tiled=T...  31.7 us
    all_to_all x1, waiting for transfers between devices, body(): lax.all_to_all(picked[0], 'expert', split_axis=0, concat_axis=0, tiled=True)  29.8 us
    all_to_all x1, waiting for transfers between devices, body(): lax.all_to_all(up_first, 'expert', split_axis=0, concat_axis=0, tiled=True)  20.7 us
    another operation x2, other arithmetic, body(): jnp.stack([jnp.stack(up_terms, axis=1), jnp.stack(down_terms, axis=1)], a...  18.9 us
  transfers between devices with their start and end apart: 9, of which 8 were waited for; matrix products, arithmetic and copies ran while one was open for 29% of the time, Pallas kernels for 0%

commit v1 on v0

v1 whole, which is shorter than its diff:
```python
import functools

import jax
import jax.numpy as jnp
from jax import lax
from jax.experimental import pallas as pl
from jax.experimental.pallas import tpu as pltpu
from jax.sharding import PartitionSpec as P

MESH = pl.DeviceIdType.MESH
BF = jnp.bfloat16
F32 = jnp.float32
DMA = pltpu.SemaphoreType.DMA
SIDE = 4


class Place:
    def __init__(self):
        self.dp = lax.axis_index("dp")
        self.me = lax.axis_index("expert")
        self.y = self.me // SIDE
        self.x = lax.rem(self.me, SIDE)

    def along_y(self, step):
        return (self.dp, lax.rem(self.y + step, SIDE) * SIDE + self.x)

    def along_x(self, step):
        return (self.dp, self.y * SIDE + lax.rem(self.x + step, SIDE))

    def first(self, half, step):
        return self.along_y(step) if half == 0 else self.along_x(step)

    def second(self, half, step):
        return self.along_x(step) if half == 0 else self.along_y(step)

    def first_at(self, half):
        return self.y if half == 0 else self.x

    def second_at(self, half):
        return self.x if half == 0 else self.y

    def greet(self):
        barrier = pltpu.get_barrier_semaphore()
        for step in (1, 2, 3):
            for peer in (self.along_y(step), self.along_x(step)):
                pl.semaphore_signal(barrier, inc=1, device_id=peer, device_id_type=MESH)
        pl.semaphore_wait(barrier, 6)


def send(src, dst, send_sem, recv_sem, peer):
    copy = pltpu.make_async_remote_copy(
        src_ref=src, dst_ref=dst, send_sem=send_sem, recv_sem=recv_sem, device_id=peer, device_id_type=MESH
    )
    copy.start()
    return copy


def dot(a, b, over_a=1, over_b=0):
    return lax.dot_general(a, b, (((over_a,), (over_b,)), ((), ())), preferred_element_type=F32)


def forth_kernel(
    cap, chosen, scale,
    route, tok, og, wu_hbm, wd_hbm,
    o_hbm, gi_hbm, dw_hbm, pick,
    rt, rank, wt, p1, st, xg, wu, wd, wbuf, wcol, slope, actw, gp, ov, gv, dwv,
    rt_s, rt_r, p1_s, p1_r, p2_s, p2_r, w_sem, o_sem, g_sem, dw_sem,
):
    at = Place()
    x, y, me = at.x, at.y, at.me
    toks = tok.shape[0]
    half_w = tok.shape[1] // 2
    hidden = wu.shape[2]
    rows = SIDE * SIDE * cap
    chunk = wbuf.shape[1]
    steps = (1, 2, 3)

    at.greet()
    rt[x * SIDE + y] = route[...]
    sends = []
    first = [
        send(route, rt.at[x * SIDE + y], rt_s.at[0, k], rt_r.at[0, k], at.along_y(k)) for k in steps
    ]

    def phase1(t):
        src = (tok, og)[t]
        out = []
        for h in (0, 1):
            for k in steps:
                out.append(
                    send(
                        src.at[:, pl.ds(h * half_w, half_w)],
                        p1.at[t, h, at.first_at(h)],
                        p1_s.at[t, h, k], p1_r.at[t, h, k], at.first(h, k),
                    )
                )
        return out

    def own1(t):
        src = (tok, og)[t]
        for h in (0, 1):
            p1[t, h, at.first_at(h)] = src[:, h * half_w : (h + 1) * half_w]

    arriving = [phase1(0), None]
    own1(0)
    for c in first:
        c.wait()
    block = rt.at[pl.ds(x * SIDE, SIDE)]
    second = [send(block, block, rt_s.at[1, k], rt_r.at[1, k], at.along_x(k)) for k in steps]

    def weights(hbm, vmem, lo, hi):
        def fetch(i):
            slot = lax.rem(i, 2)
            return pltpu.make_async_copy(
                hbm.at[pl.ds(pl.multiple_of(i * chunk, chunk), chunk)], wbuf.at[slot], w_sem.at[slot]
            )

        fetch(lo).start()

        def turn(i, carry):
            @pl.when(i + 1 < hi)
            def _():
                fetch(i + 1).start()

            fetch(i).wait()
            vmem[:, pl.ds(pl.multiple_of(i * chunk, chunk), chunk), :] = jnp.swapaxes(
                wbuf[lax.rem(i, 2)], 0, 1
            )
            return carry

        lax.fori_loop(lo, hi, turn, 0)

    n_chunks = wu.shape[1] // chunk
    for c in second:
        c.wait()

    before = (
        lax.broadcasted_iota(jnp.int32, (toks, toks), 0) < lax.broadcasted_iota(jnp.int32, (toks, toks), 1)
    ).astype(F32).astype(BF)
    n_exp = rank.shape[1]
    owners = n_exp // 2
    line = lax.broadcasted_iota(jnp.int32, (n_exp, toks), 0)
    expert = (lax.rem(line, owners) * 2 + line // owners).astype(F32)

    def ranks(n, carry):
        r = rt[n]
        named = jnp.zeros((n_exp, toks), F32)
        weight = jnp.zeros((n_exp, toks), F32)
        for k in range(chosen):
            m = (r[k : k + 1, :] == expert).astype(F32)
            named += m
            weight += m * r[8 + k : 9 + k, :]
        pos = dot(named.astype(BF), before)
        rank[n] = jnp.where(named > 0, pos, -1.0)
        wt[n] = weight
        return carry

    lax.fori_loop(0, SIDE * SIDE, ranks, 0)
    place = lax.broadcasted_iota(jnp.int32, (cap, toks), 0).astype(F32)

    def picks(j, carry):
        for h in (0, 1):
            n = x * SIDE + j if h == 0 else j * SIDE + y
            for s in (0, 1):
                for d in range(SIDE):
                    owner = y * SIDE + d if h == 0 else d * SIDE + x
                    q = rank[n, pl.ds(s * owners + owner, 1), :]
                    pick[h, j, (s * SIDE + d) * cap : (s * SIDE + d + 1) * cap, :] = (
                        (place == q).astype(F32).astype(BF)
                    )
        return carry

    lax.fori_loop(0, SIDE, picks, 0)

    def slot_weights(n, carry):
        for s in (0, 1):
            q = rank[n, pl.ds(s * owners + me, 1), :]
            w = wt[n, pl.ds(s * owners + me, 1), :]
            col = jnp.sum(jnp.where(place == q, w, 0.0), axis=1, keepdims=True)
            row = (lax.rem(n, SIDE) * SIDE + n // SIDE) * cap
            wcol[s, pl.ds(pl.multiple_of(row, cap), cap), :] = jnp.broadcast_to(col, (cap, toks))
        return carry

    lax.fori_loop(0, SIDE * SIDE, slot_weights, 0)

    weights(wu_hbm, wu, 0, n_chunks // 2)
    arriving[1] = phase1(1)
    own1(1)
    weights(wu_hbm, wu, n_chunks // 2, n_chunks)

    def stage(t):
        for h in (0, 1):
            mine = at.second_at(h)

            def turn(j, carry):
                got = dot(pick[h, j], p1[t, h, j]).astype(BF).reshape(2, SIDE, cap, half_w)
                st[t, h, :, :, j] = got
                return carry

            lax.fori_loop(0, SIDE, turn, 0)
            for s in (0, 1):
                own = st[t, h, s, pl.ds(mine, 1)].reshape(SIDE, cap, half_w)
                if h == 0:
                    xg[t, s, h, :, pl.ds(x, 1)] = own.reshape(SIDE, 1, cap, half_w)
                else:
                    xg[t, s, h, pl.ds(y, 1)] = own.reshape(1, SIDE, cap, half_w)

    def phase2(t, s):
        out = []
        for h in (0, 1):
            for k in steps:
                peer_at = lax.rem(at.second_at(h) + k, SIDE)
                dst = xg.at[t, s, h, :, x] if h == 0 else xg.at[t, s, h, y]
                out.append(
                    send(st.at[t, h, s, peer_at], dst, p2_s.at[t, s, h, k], p2_r.at[t, s, h, k], at.second(h, k))
                )
        return out

    moving = {}
    for c in arriving[0]:
        c.wait_recv()
    stage(0)
    moving[0, 0] = phase2(0, 0)
    for c in arriving[1]:
        c.wait_recv()
    stage(1)
    moving[1, 0] = phase2(1, 0)
    moving[0, 1] = phase2(0, 1)
    moving[1, 1] = phase2(1, 1)
    weights(wd_hbm, wd, 0, n_chunks)

    tile = 256
    h_tiles = hidden // tile
    d_tiles = 2 * half_w // tile
    per_half = half_w // tile

    def inputs(t, s, h):
        return xg[t, s, h].reshape(rows, half_w)

    def forward(s):
        def turn(n, carry):
            cols = pl.ds(pl.multiple_of(n * tile, tile), tile)
            pre = dot(inputs(0, s, 0), wu[s, 0:half_w, cols]) + dot(inputs(0, s, 1), wu[s, half_w : 2 * half_w, cols])
            w = wcol[s, :, 0:1]
            sig = 1.0 / (1.0 + jnp.exp(-pre))
            actw[s, :, cols] = (pre * sig * w).astype(BF)
            slope[s, :, cols] = sig * (1.0 + pre * (1.0 - sig)) * w
            return carry

        lax.fori_loop(0, h_tiles, turn, 0)

        def out(i, carry):
            got = dot(actw[s], wd[s, pl.ds(pl.multiple_of(i * tile, tile), tile), :], 1, 1)
            ov[s, i // per_half, :, pl.ds(pl.multiple_of(lax.rem(i, per_half) * tile, tile), tile)] = got.astype(BF)
            return carry

        lax.fori_loop(0, d_tiles, out, 0)
        copy = pltpu.make_async_copy(ov.at[s], o_hbm.at[s], o_sem.at[s])
        copy.start()
        return copy

    def backward(s):
        def turn(n, carry):
            cols = pl.ds(pl.multiple_of(n * tile, tile), tile)
            ga = dot(inputs(1, s, 0), wd[s, 0:half_w, cols]) + dot(inputs(1, s, 1), wd[s, half_w : 2 * half_w, cols])
            gp[s, :, cols] = (ga * slope[s, :, cols]).astype(BF)
            return carry

        lax.fori_loop(0, h_tiles, turn, 0)

        def grad(i, carry):
            got = dot(gp[s], wu[s, pl.ds(pl.multiple_of(i * tile, tile), tile), :], 1, 1)
            gv[s, i // per_half, :, pl.ds(pl.multiple_of(lax.rem(i, per_half) * tile, tile), tile)] = got.astype(BF)
            return carry

        def drain(t, i):
            slot = lax.rem(i, 2)
            return pltpu.make_async_copy(
                dwv.at[t, slot],
                dw_hbm.at[s, pl.ds(pl.multiple_of(i * tile, tile), tile), pl.ds(t * hidden, hidden)],
                dw_sem.at[t, slot],
            )

        def dw(i, carry):
            cols = pl.ds(pl.multiple_of(lax.rem(i, per_half) * tile, tile), tile)
            for t, other in ((0, gp), (1, actw)):
                left = xg[t, s, i // per_half, :, :, :, cols].reshape(rows, tile)
                got = dot(left, other[s], 0, 0) * scale

                @pl.when(i >= 2)
                def _():
                    drain(t, i - 2).wait()

                dwv[t, lax.rem(i, 2)] = got.astype(BF)
                drain(t, i).start()
            return carry

        lax.fori_loop(0, d_tiles, dw, 0)
        for i in (d_tiles - 2, d_tiles - 1):
            for t in (0, 1):
                drain(t, i).wait()
        lax.fori_loop(0, d_tiles, grad, 0)
        copy = pltpu.make_async_copy(gv.at[s], gi_hbm.at[s], g_sem.at[s])
        copy.start()
        return copy

    local = []
    for s in (0, 1):
        for c in moving[0, s]:
            c.wait_recv()
        local.append(forward(s))
        for c in moving[1, s]:
            c.wait_recv()
        local.append(backward(s))
    for c in arriving[0] + arriving[1]:
        c.wait_send()
    for t in (0, 1):
        for s in (0, 1):
            for c in moving[t, s]:
                c.wait_send()
    for c in local:
        c.wait()


def back_kernel(cap, o_hbm, gi_hbm, pick, out, ig, rec, dense, part, own_sem, r1_s, r1_r, r2_s, r2_r):
    at = Place()
    steps = (1, 2, 3)
    half_w = out.shape[1] // 2
    toks = out.shape[0]
    at.greet()

    def block(t, s, h, other):
        src = (o_hbm, gi_hbm)[t]
        return src.at[s, h, :, other] if h == 0 else src.at[s, h, other]

    def phase1(t, s):
        copies = []
        for h in (0, 1):
            mine = at.second_at(h)
            dst = rec.at[t, h, :, s, mine]
            own = pltpu.make_async_copy(block(t, s, h, mine), dst, own_sem.at[t, s, h])
            own.start()
            for k in steps:
                peer_at = lax.rem(mine + k, SIDE)
                copies.append(
                    send(block(t, s, h, peer_at), dst, r1_s.at[t, s, h, k], r1_r.at[t, s, h, k], at.second(h, k))
                )
            copies.append(own)
        return copies

    def arrived(copies):
        for c in copies:
            if c.is_remote:
                c.wait_recv()
            else:
                c.wait()

    def token_sums(t, h, j):
        return dot(pick[h, j], rec[t, h, j].reshape(2 * SIDE * cap, half_w), 0, 0)

    moving = {}
    second = {0: [], 1: []}

    def phase2(t):
        for h in (0, 1):
            mine = at.first_at(h)
            for k in steps:
                j = lax.rem(mine + k, SIDE)
                dense[t, h, k - 1] = token_sums(t, h, j).astype(BF)
                second[t].append(
                    send(dense.at[t, h, k - 1], part.at[t, h, k - 1], r2_s.at[t, h, k], r2_r.at[t, h, k], at.first(h, k))
                )

    def finish(t):
        result = (out, ig)[t]
        for h in (0, 1):
            total = token_sums(t, h, at.first_at(h))
            for c in second[t][3 * h : 3 * h + 3]:
                c.wait_recv()
            for k in steps:
                total = total + part[t, h, k - 1].astype(F32)
            result[:, h * half_w : (h + 1) * half_w] = total.astype(BF)

    moving[0, 0] = phase1(0, 0)
    moving[0, 1] = phase1(0, 1)
    arrived(moving[0, 0])
    moving[1, 0] = phase1(1, 0)
    arrived(moving[0, 1])
    moving[1, 1] = phase1(1, 1)
    phase2(0)
    arrived(moving[1, 0])
    arrived(moving[1, 1])
    phase2(1)
    finish(0)
    finish(1)
    for copies in list(moving.values()) + list(second.values()):
        for c in copies:
            if c.is_remote:
                c.wait_send()


def body(tokens, expert_ids, combine_weight, partner, w_up, w_down, out_grad):
    toks, chosen = expert_ids.shape
    width = tokens.shape[1]
    half_w = width // 2
    hidden = w_up.shape[2]
    owners = SIDE * SIDE
    cap = toks * chosen * 4 // (3 * 2 * owners)
    rows = owners * cap
    pad = jnp.zeros((8 - chosen, toks), F32)
    route = jnp.concatenate([expert_ids.T.astype(F32), pad, combine_weight.T, pad], axis=0)
    any_ = pl.BlockSpec(memory_space=pl.ANY)
    vmem = pl.BlockSpec(memory_space=pltpu.VMEM)
    o_buf, gi_buf, dw, pick = pl.pallas_call(
        functools.partial(forth_kernel, cap, chosen, 1.0 / toks),
        out_shape=(
            jax.ShapeDtypeStruct((2, 2, rows, half_w), BF),
            jax.ShapeDtypeStruct((2, 2, rows, half_w), BF),
            jax.ShapeDtypeStruct((2, width, 2 * hidden), BF),
            jax.ShapeDtypeStruct((2, SIDE, 2 * SIDE * cap, toks), BF),
        ),
        in_specs=[vmem, vmem, vmem, any_, any_],
        out_specs=(any_, any_, any_, vmem),
        scratch_shapes=[
            pltpu.VMEM((owners, 16, toks), F32),
            pltpu.VMEM((owners, 2 * owners, toks), F32),
            pltpu.VMEM((owners, 2 * owners, toks), F32),
            pltpu.VMEM((2, 2, SIDE, toks, half_w), BF),
            pltpu.VMEM((2, 2, 2, SIDE, SIDE, cap, half_w), BF),
            pltpu.VMEM((2, 2, 2, SIDE, SIDE, cap, half_w), BF),
            pltpu.VMEM((2, width, hidden), BF),
            pltpu.VMEM((2, width, hidden), BF),
            pltpu.VMEM((2, 128, 2, hidden), BF),
            pltpu.VMEM((2, rows, toks), F32),
            pltpu.VMEM((2, rows, hidden), F32),
            pltpu.VMEM((2, rows, hidden), BF),
            pltpu.VMEM((2, rows, hidden), BF),
            pltpu.VMEM((2, 2, rows, half_w), BF),
            pltpu.VMEM((2, 2, rows, half_w), BF),
            pltpu.VMEM((2, 2, 256, hidden), BF),
            DMA((2, 4)), DMA((2, 4)),
            DMA((2, 2, 4)), DMA((2, 2, 4)),
            DMA((2, 2, 2, 4)), DMA((2, 2, 2, 4)),
            DMA((2,)), DMA((2,)), DMA((2,)), DMA((2, 2)),
        ],
        compiler_params=pltpu.CompilerParams(
            collective_id=0, has_side_effects=True, vmem_limit_bytes=60 << 20
        ),
    )(route, tokens, out_grad, w_up, w_down)

    summed = [lax.psum_scatter(dw[s], "dp", scatter_dimension=0, tiled=True) for s in (0, 1)]

    shape = (2, 2, SIDE, SIDE, cap, half_w)
    output, input_grad = pl.pallas_call(
        functools.partial(back_kernel, cap),
        out_shape=(
            jax.ShapeDtypeStruct((toks, width), BF),
            jax.ShapeDtypeStruct((toks, width), BF),
        ),
        in_specs=[any_, any_, vmem],
        out_specs=(vmem, vmem),
        scratch_shapes=[
            pltpu.VMEM((2, 2, SIDE, 2, SIDE, cap, half_w), BF),
            pltpu.VMEM((2, 2, SIDE - 1, toks, half_w), BF),
            pltpu.VMEM((2, 2, SIDE - 1, toks, half_w), BF),
            DMA((2, 2, 2)),
            DMA((2, 2, 2, 4)), DMA((2, 2, 2, 4)),
            DMA((2, 2, 4)), DMA((2, 2, 4)),
        ],
        compiler_params=pltpu.CompilerParams(
            collective_id=1, has_side_effects=True, vmem_limit_bytes=40 << 20
        ),
    )(o_buf.reshape(shape), gi_buf.reshape(shape), pick)

    n_rows = summed[0].shape[0]
    spread = lax.all_to_all(
        summed[0].reshape(owners, n_rows // owners, 2 * hidden), "expert", split_axis=0, concat_axis=0, tiled=True
    )
    choose = (partner[:, None] == jnp.arange(owners, dtype=jnp.int32)[None, :]).astype(BF)
    ordered = lax.dot_general(
        choose, spread, (((1,), (0,)), ((), ())), preferred_element_type=F32
    ).astype(BF)
    moved = lax.all_to_all(ordered, "expert", split_axis=0, concat_axis=0, tiled=True).reshape(n_rows, 2 * hidden)
    grad_up = jnp.stack([moved[:, :hidden], summed[1][:, :hidden]], axis=1)
    grad_down = jnp.stack([moved[:, hidden:], summed[1][:, hidden:]], axis=1)
    return (output, input_grad, grad_up, grad_down)


def solution(mesh):
    return jax.shard_map(
        body,
        mesh=mesh,
        in_specs=(
            P(("dp", "expert"), None),
            P(("dp", "expert"), None),
            P(("dp", "expert"), None),
            P(),
            P(None, "expert", None),
            P(None, "expert", None),
            P(("dp", "expert"), None),
        ),
        out_specs=(
            P(("dp", "expert"), None),
            P(("dp", "expert"), None),
            P("dp", "expert", None),
            P("dp", "expert", None),
        ),
        check_vma=False,
    )
```

time: 570 us -> 288 us (0.51); the launches traced: 560 us -> 286 us
  waiting for transfers between devices: 274 us -> 43.4 us
  Pallas kernels: 0 us -> 179 us
  local copies, waits for them, and re-layouts: 114 us -> 22.3 us
  other arithmetic: 65.6 us -> 2.12 us
  matrix products: 52.2 us -> 0.64 us
  starting transfers between devices: 39.5 us -> 3.88 us
  blocking collectives: 0 us -> 20.4 us
    all_to_all x8 -> x1, waiting for transfers between devices: 274 us -> 0.01 us  [body(): lax.all_to_all(ordered, 'expert', split_axis=0, concat_axis=0, tiled=True)]
    pallas_call x0 -> x2, Pallas kernels: none -> 179 us  [the longest x1 104 us: body(): pl.pallas_call(functools.partial(forth_kernel, cap, chosen, 1.0 / toks),...]
    dot_general x12 -> x1, matrix products: 52.2 us -> 0.64 us  [body(): lax.dot_general(choose, spread, (((1,), (0,)), ((), ())), preferred_eleme...]
    reduce_scatter x1 -> x2, waiting for transfers between devices: 0.01 us -> 42.7 us  [body(): lax.psum_scatter(dw[s], 'dp', scatter_dimension=0, tiled=True)]
    gather x7 -> x0, local copies, waits for them, and re-layouts: 37.7 us -> none  [the longest x1 9.06 us: body(): returned[flat_slot].reshape(tok_dev, chosen, model_width)]
    slice x5 -> x0, local copies, waits for them, and re-layouts: 36.9 us -> none  [the longest x1 13.6 us: body(): up_first = w_up[:, 0, :].reshape(owners, model_width // owners, hidden)]
    all_to_all x8 -> x1, starting transfers between devices: 39.3 us -> 3.8 us  [body(): lax.all_to_all(ordered, 'expert', split_axis=0, concat_axis=0, tiled=True)]
    another operation x6 -> x1, other arithmetic: 25.3 us -> 0.14 us  [body(): grad_up = jnp.stack([moved[:, :hidden], summed[1][:, :hidden]], axis=1)]
  transfers between devices with their start and end apart: 9 -> 3, of which waited for: 8 -> 1; matrix products, arithmetic and copies ran while one was open for 29% -> 1% of each run, Pallas kernels for 0% -> 26%
where the time goes in v1:
time: 288 us; the launch traced here: 286 us
  Pallas kernels  179 us (62%)
  waiting for transfers between devices  43.4 us (15%)
  local copies, waits for them, and re-layouts  22.3 us (8%)
  blocking collectives  20.4 us (7%)
  between operations  14.1 us (5%)
  starting transfers between devices  3.88 us (1%)
    pallas_call x1, Pallas kernels, body(): pl.pallas_call(functools.partial(forth_kernel, cap, chosen, 1.0 / toks),...  104 us
    pallas_call x1, Pallas kernels, body(): pl.pallas_call(functools.partial(back_kernel, cap), out_shape=(jax.ShapeD...  75.8 us
    reduce_scatter x2, waiting for transfers between devices, body(): lax.psum_scatter(dw[s], 'dp', scatter_dimension=0, tiled=True)  42.7 us
    all_to_all x1, blocking collectives, body(): lax.all_to_all(summed[0].reshape(owners, n_rows // owners, 2 * hidden), '...  20.4 us
    squeeze x1, local copies, waits for them, and re-layouts, body(): dw[s]  10.2 us
    unnamed x12, local copies, waits for them, and re-layouts  9.53 us
  transfers between devices with their start and end apart: 3, of which 1 were waited for; matrix products, arithmetic and copies ran while one was open for 1% of the time, Pallas kernels for 26%

profile of v1, /device:TPU:0, one launch (start us, length us, event | category | flops | bytes accessed | tf_op | source)
XLA Modules:
  0.0 286.3 jit_solution(4507949389655477749)
XLA Ops:
  7.2 0.0 reduce-scatter.3.cloned.1.call-start
  7.2 0.7 convert_bitcast_fusion
  7.9 1.3 pad_maximum_fusion.2.route
  9.2 103.5 %shard_map.102 = (bf16[2,2,512,1024]{3,2,1,0:T(8,128)(2,1)}, bf16[2,2,512,1024]{3,2,1,0:T(8,128)(2,1)}, bf16[2,2048,1536]{2,1,0:T(8,128)(2,1)}, bf16[2,4,256,128]{3,2,1,0:T(8,128)(2,1)}) custom-call(f32[16,128]{1,0:T(8,128)} %pad_maximum_fusion.2.route, bf16[128,2048]{1,0:T(8,128)(2,1)} %tok.1, bf16[128,2048]{1,0:T(8,128)(2,1)} %og.1, ...), custom_call_target="tpu_custom_call" | custom-call | tf_op jit(solution)/shard_map/pallas_call | solution.py:414
  112.7 10.2 %slice_bitcast_fusion.1 = (bf16[2048,1536]{1,0:T(8,128)(2,1)}, bf16[2048,1536]{1,0:T(8,128)(2,1)}) fusion(bf16[2,2048,1536]{2,1,0:T(8,128)(2,1)} %get-tuple-element.15), kind=kLoop, calls=%fused_computation.1 | loop fusion | bytes 25165824 | tf_op jit(solution)/shard_map/squeeze | solution.py:451
  122.9 0.0 copy-start.3
  122.9 0.0 reduce-scatter.3.cloned.1.call-update
  123.0 0.0 reduce-scatter.5.cloned.1.call-start
  123.0 0.0 copy-start.2
  123.0 0.7 reduce-scatter.5.cloned.1.call-update
  123.7 42.7 %reduce-scatter.3.cloned.1.call-done = bf16[256,1536]{1,0:T(8,128)(2,1)} async-done(((bf16[2048,1536]{1,0:T(8,128)(2,1)}), bf16[256,1536]{1,0:T(8,128)(2,1)}) %reduce-scatter.3.cloned.1.call-update) | async-done | bytes 786448 | tf_op jit(solution)/shard_map/reduce_scatter | solution.py:451
  166.4 20.4 %all_to_all.10 = bf16[16,16,1536]{2,1,0:T(8,128)(2,1)S(1)} all-to-all(bf16[16,16,1536]{2,1,0:T(8,128)(2,1)} %bitcast.25), channel_id=1, replica_groups=mesh['dp'=8,'expert'=16] {'expert'}, dimensions={0} | all-to-all | bytes 1572864 | tf_op jit(solution)/shard_map/all_to_all | solution.py:476
  186.9 0.0 copy-done.3
  186.9 0.6 convolution_convert_fusion
  187.5 1.3 copy.16
  188.8 3.8 %all-to-all-start.1 = ((bf16[16,16,1536]{2,1,0:T(8,128)(2,1)}), bf16[16,16,1536]{2,1,0:T(8,128)(2,1)S(1)}, u32[]{:S(2)}, u32[]{:S(2)}) async-start(bf16[16,16,1536]{2,1,0:T(8,128)(2,1)} %copy.16), calls=%async_computation.2 | async-start | bytes 1572864 | tf_op jit(solution)/shard_map/all_to_all | solution.py:483
  192.7 0.0 copy-done.2
  192.7 0.0 copy-start
  192.7 2.3 copy-done
  195.0 0.0 copy-start.1
  195.0 2.3 copy-done.1
  197.2 75.8 %shard_map.103 = (bf16[128,2048]{1,0:T(8,128)(2,1)S(1)}, bf16[128,2048]{1,0:T(8,128)(2,1)S(1)}) custom-call(bf16[2,2,4,4,32,1024]{5,4,3,2,1,0:T(8,128)(2,1)S(1)} %bitcast.22, bf16[2,2,4,4,32,1024]{5,4,3,2,1,0:T(8,128)(2,1)S(1)} %bitcast.23, bf16[2,4,256,128]{3,2,1,0:T(8,128)(2,1)S(1)} %copy-done.2), custom_call_target="tpu_custom_call" | custom-call | tf_op jit(solution)/shard_map/pallas_call | solution.py:454
  273.0 0.0 reduce-scatter.5.cloned.1.call-done
  273.1 1.2 slice_bitcast_fusion.2
  274.2 0.0 all-to-all-done.1
  274.2 0.1 slice_bitcast_fusion.3
  274.3 0.1 pad_maximum_fusion
  274.5 1.7 copy.17
  276.1 1.7 copy.18
  277.8 0.8 copy.23
  278.6 0.8 copy.24
  (1 shorter events, 0.0 us)
Async XLA Ops:
  7.2 159.3 %reduce-scatter.3.cloned.1.call-start = ((), (), s32[]{:S(2)}) async-start(), calls=%async_computation.4 | async-start | bytes 7077888 | tf_op jit(solution)/shard_map/reduce_scatter | solution.py:451
  122.9 63.9 %copy-start.3 = (s32[16]{0:T(128)S(1)}, s32[16]{0:T(128)}, u32[]{:S(2)}) copy-start(s32[16]{0:T(128)} %param.10) | copy-start | bytes 196
  123.0 150.1 %reduce-scatter.5.cloned.1.call-start = ((), (), s32[]{:S(2)}) async-start(), calls=%async_computation.5 | async-start | bytes 7077888 | tf_op jit(solution)/shard_map/reduce_scatter | solution.py:451
  123.0 69.6 %copy-start.2 = (bf16[2,4,256,128]{3,2,1,0:T(8,128)(2,1)S(1)}, bf16[2,4,256,128]{3,2,1,0:T(8,128)(2,1)}, u32[]{:S(2)}) copy-start(bf16[2,4,256,128]{3,2,1,0:T(8,128)(2,1)} %get-tuple-element.12.pick) | copy-start | bytes 1572868
  188.8 85.4 %all-to-all-start.1 = ((bf16[16,16,1536]{2,1,0:T(8,128)(2,1)}), bf16[16,16,1536]{2,1,0:T(8,128)(2,1)S(1)}, u32[]{:S(2)}, u32[]{:S(2)}) async-start(bf16[16,16,1536]{2,1,0:T(8,128)(2,1)} %copy.16), calls=%async_computation.2 | async-start | bytes 1572864 | tf_op jit(solution)/shard_map/all_to_all | solution.py:483
  192.7 2.3 copy-start
  195.0 2.3 copy-start.1
Sparse Core Ops, SparseCore 0:
  123.1 43.3 reduce-scatter.2
  168.9 42.3 reduce-scatter.4

commit v2 on v1

v2 whole, which is shorter than its diff:
```python
import functools

import jax
import jax.numpy as jnp
from jax import lax
from jax.experimental import pallas as pl
from jax.experimental.pallas import tpu as pltpu
from jax.sharding import PartitionSpec as P

MESH = pl.DeviceIdType.MESH
BF = jnp.bfloat16
F32 = jnp.float32
DMA = pltpu.SemaphoreType.DMA
SIDE = 4


class Place:
    def __init__(self):
        self.dp = lax.axis_index("dp")
        self.me = lax.axis_index("expert")
        self.y = self.me // SIDE
        self.x = lax.rem(self.me, SIDE)
        self.z = self.dp // 2
        self.core = lax.rem(self.dp, 2)

    def along_y(self, step):
        return (self.dp, lax.rem(self.y + step, SIDE) * SIDE + self.x)

    def along_x(self, step):
        return (self.dp, self.y * SIDE + lax.rem(self.x + step, SIDE))

    def first(self, half, step):
        return self.along_y(step) if half == 0 else self.along_x(step)

    def second(self, half, step):
        return self.along_x(step) if half == 0 else self.along_y(step)

    def first_at(self, half):
        return self.y if half == 0 else self.x

    def second_at(self, half):
        return self.x if half == 0 else self.y

    def along_z(self, step):
        return (lax.rem(self.z + step, SIDE) * 2 + self.core, self.me)

    def other_core(self):
        return (self.z * 2 + 1 - self.core, self.me)

    def greet(self):
        barrier = pltpu.get_barrier_semaphore()
        peers = [self.other_core()]
        for step in (1, 2, 3):
            peers += [self.along_y(step), self.along_x(step), self.along_z(step)]
        for peer in peers:
            pl.semaphore_signal(barrier, inc=1, device_id=peer, device_id_type=MESH)
        pl.semaphore_wait(barrier, len(peers))


def send(src, dst, send_sem, recv_sem, peer):
    copy = pltpu.make_async_remote_copy(
        src_ref=src, dst_ref=dst, send_sem=send_sem, recv_sem=recv_sem, device_id=peer, device_id_type=MESH
    )
    copy.start()
    return copy


def dot(a, b, over_a=1, over_b=0):
    return lax.dot_general(a, b, (((over_a,), (over_b,)), ((), ())), preferred_element_type=F32)


def kernel(
    cap, chosen, scale,
    route, tok, og, wu_hbm, wd_hbm,
    out, ig, g0_hbm, g1_hbm, rec, cr, zr,
    rt, rank, wt, pick, p1, st, xg, wu, wd, wbuf, wcol, slope, right, part, rbuf, own, xs, ld,
    rt_s, rt_r, p1_s, p1_r, p2_s, p2_r, w_sem, r1_s, r1_r, own_sem, r2_s, r2_r, rb_sem,
    c_s, c_r, z_s, z_r, ld_sem, g_sem,
):
    at = Place()
    x, y, me = at.x, at.y, at.me
    toks = tok.shape[0]
    half_w = tok.shape[1] // 2
    hidden = wu.shape[2]
    rows = SIDE * SIDE * cap
    chunk = wbuf.shape[1]
    steps = (1, 2, 3)

    at.greet()
    rt[x * SIDE + y] = route[...]
    sends = []
    first = [
        send(route, rt.at[x * SIDE + y], rt_s.at[0, k], rt_r.at[0, k], at.along_y(k)) for k in steps
    ]

    def phase1(t):
        src = (tok, og)[t]
        out = []
        for h in (0, 1):
            for k in steps:
                out.append(
                    send(
                        src.at[:, pl.ds(h * half_w, half_w)],
                        p1.at[t, h, at.first_at(h)],
                        p1_s.at[t, h, k], p1_r.at[t, h, k], at.first(h, k),
                    )
                )
        return out

    def own1(t):
        src = (tok, og)[t]
        for h in (0, 1):
            p1[t, h, at.first_at(h)] = src[:, h * half_w : (h + 1) * half_w]

    arriving = [phase1(0), None]
    own1(0)
    for c in first:
        c.wait()
    block = rt.at[pl.ds(x * SIDE, SIDE)]
    second = [send(block, block, rt_s.at[1, k], rt_r.at[1, k], at.along_x(k)) for k in steps]

    def weights(hbm, vmem, lo, hi):
        def fetch(i):
            slot = lax.rem(i, 2)
            return pltpu.make_async_copy(
                hbm.at[pl.ds(pl.multiple_of(i * chunk, chunk), chunk)], wbuf.at[slot], w_sem.at[slot]
            )

        fetch(lo).start()

        def turn(i, carry):
            @pl.when(i + 1 < hi)
            def _():
                fetch(i + 1).start()

            fetch(i).wait()
            vmem[:, pl.ds(pl.multiple_of(i * chunk, chunk), chunk), :] = jnp.swapaxes(
                wbuf[lax.rem(i, 2)], 0, 1
            )
            return carry

        lax.fori_loop(lo, hi, turn, 0)

    n_chunks = wu.shape[1] // chunk
    for c in second:
        c.wait()

    before = (
        lax.broadcasted_iota(jnp.int32, (toks, toks), 0) < lax.broadcasted_iota(jnp.int32, (toks, toks), 1)
    ).astype(F32).astype(BF)
    n_exp = rank.shape[1]
    owners = n_exp // 2
    line = lax.broadcasted_iota(jnp.int32, (n_exp, toks), 0)
    expert = (lax.rem(line, owners) * 2 + line // owners).astype(F32)

    def ranks(n, carry):
        r = rt[n]
        named = jnp.zeros((n_exp, toks), F32)
        weight = jnp.zeros((n_exp, toks), F32)
        for k in range(chosen):
            m = (r[k : k + 1, :] == expert).astype(F32)
            named += m
            weight += m * r[8 + k : 9 + k, :]
        pos = dot(named.astype(BF), before)
        rank[n] = jnp.where(named > 0, pos, -1.0)
        wt[n] = weight
        return carry

    lax.fori_loop(0, SIDE * SIDE, ranks, 0)
    place = lax.broadcasted_iota(jnp.int32, (cap, toks), 0).astype(F32)

    def picks(j, carry):
        for h in (0, 1):
            n = x * SIDE + j if h == 0 else j * SIDE + y
            for s in (0, 1):
                for d in range(SIDE):
                    owner = y * SIDE + d if h == 0 else d * SIDE + x
                    q = rank[n, pl.ds(s * owners + owner, 1), :]
                    pick[h, j, (s * SIDE + d) * cap : (s * SIDE + d + 1) * cap, :] = (
                        (place == q).astype(F32).astype(BF)
                    )
        return carry

    lax.fori_loop(0, SIDE, picks, 0)

    def slot_weights(n, carry):
        for s in (0, 1):
            q = rank[n, pl.ds(s * owners + me, 1), :]
            w = wt[n, pl.ds(s * owners + me, 1), :]
            col = jnp.sum(jnp.where(place == q, w, 0.0), axis=1, keepdims=True)
            row = (lax.rem(n, SIDE) * SIDE + n // SIDE) * cap
            wcol[s, pl.ds(pl.multiple_of(row, cap), cap), :] = jnp.broadcast_to(col, (cap, toks))
        return carry

    lax.fori_loop(0, SIDE * SIDE, slot_weights, 0)

    weights(wu_hbm, wu, 0, n_chunks // 4)
    arriving[1] = phase1(1)
    own1(1)
    weights(wu_hbm, wu, n_chunks // 4, n_chunks)

    def stage(t):
        for h in (0, 1):
            mine = at.second_at(h)

            def turn(j, carry):
                got = dot(pick[h, j], p1[t, h, j]).astype(BF).reshape(2, SIDE, cap, half_w)
                st[t, h, :, :, j] = got
                return carry

            lax.fori_loop(0, SIDE, turn, 0)
            for s in (0, 1):
                own = st[t, h, s, pl.ds(mine, 1)].reshape(SIDE, cap, half_w)
                if h == 0:
                    xg[t, s, h, :, pl.ds(x, 1)] = own.reshape(SIDE, 1, cap, half_w)
                else:
                    xg[t, s, h, pl.ds(y, 1)] = own.reshape(1, SIDE, cap, half_w)

    def phase2(t, s):
        out = []
        for h in (0, 1):
            for k in steps:
                peer_at = lax.rem(at.second_at(h) + k, SIDE)
                dst = xg.at[t, s, h, :, x] if h == 0 else xg.at[t, s, h, y]
                out.append(
                    send(st.at[t, h, s, peer_at], dst, p2_s.at[t, s, h, k], p2_r.at[t, s, h, k], at.second(h, k))
                )
        return out

    moving = {}
    for c in arriving[0]:
        c.wait_recv()
    stage(0)
    moving[0, 0] = phase2(0, 0)
    weights(wd_hbm, wd, 0, n_chunks // 2)
    for c in arriving[1]:
        c.wait_recv()
    stage(1)
    moving[1, 0] = phase2(1, 0)
    moving[0, 1] = phase2(0, 1)
    moving[1, 1] = phase2(1, 1)
    weights(wd_hbm, wd, n_chunks // 2, n_chunks)

    tile = 256
    h_tiles = hidden // tile
    d_tiles = 2 * half_w // tile
    per_half = half_w // tile

    def inputs(t, s, h):
        return xg[t, s, h].reshape(rows, half_w)

    def put(i, got, dst):
        cols = pl.ds(pl.multiple_of(lax.rem(i, per_half) * tile, tile), tile)
        dst[i // per_half, :, :, :, cols] = got.astype(BF).reshape(SIDE, SIDE, cap, tile)

    def forward(s):
        def turn(n, carry):
            cols = pl.ds(pl.multiple_of(n * tile, tile), tile)
            pre = dot(inputs(0, s, 0), wu[s, 0:half_w, cols]) + dot(inputs(0, s, 1), wu[s, half_w : 2 * half_w, cols])
            w = wcol[s, :, 0:1]
            sig = 1.0 / (1.0 + jnp.exp(-pre))
            right[1, s, :, cols] = (pre * sig * w).astype(BF)
            slope[s, :, cols] = sig * (1.0 + pre * (1.0 - sig)) * w
            return carry

        lax.fori_loop(0, h_tiles, turn, 0)
        for c in moving[0, s]:
            c.wait_send()

        def result(i, carry):
            put(i, dot(right[1, s], wd[s, pl.ds(pl.multiple_of(i * tile, tile), tile), :], 1, 1), st.at[0, :, s])
            return carry

        lax.fori_loop(0, d_tiles, result, 0)

    def core_copy(s, n, zz):
        return pltpu.make_async_remote_copy(
            src_ref=xs.at[n % 2], dst_ref=cr.at[s, zz], send_sem=c_s.at[s, n], recv_sem=c_r.at[s, n],
            device_id=at.other_core(), device_id_type=MESH,
        )

    def gradient_tile(s, i, dst):
        cols = pl.ds(pl.multiple_of(lax.rem(i, per_half) * tile, tile), tile)

        def turn(t, carry):
            left = xg[t, s, i // per_half, :, :, :, cols].reshape(rows, tile)
            got = dot(left, right[t, s], 0, 0) * scale
            dst[:, pl.ds(pl.multiple_of(t * hidden, 128), hidden)] = got.astype(BF)
            return carry

        lax.fori_loop(0, 2, turn, 0)

    quarters = (2, 1, 3, 0)
    z_moving = {0: [], 1: []}

    def pair_sum(s, n):
        step = quarters[n]
        zz = lax.rem(at.z + step, SIDE)
        own[s, zz] = (own[s, zz].astype(F32) + ld[n % 2].astype(F32)).astype(BF)
        if step:
            z_moving[s].append(
                send(own.at[s, zz], zr.at[s, step - 1], z_s.at[s, step], z_r.at[s, step], at.along_z(step))
            )

    def fetch_pair(s, n):
        zz = lax.rem(at.z + quarters[n], SIDE)
        core_copy(s, n, zz).wait_recv()
        copy = pltpu.make_async_copy(cr.at[s, zz], ld.at[n % 2], ld_sem.at[n % 2])
        copy.start()
        return copy

    def backward(s):
        def turn(n, carry):
            cols = pl.ds(pl.multiple_of(n * tile, tile), tile)
            ga = dot(inputs(1, s, 0), wd[s, 0:half_w, cols]) + dot(inputs(1, s, 1), wd[s, half_w : 2 * half_w, cols])
            right[0, s, :, cols] = (ga * slope[s, :, cols]).astype(BF)
            return carry

        lax.fori_loop(0, h_tiles, turn, 0)
        for n, step in enumerate(quarters):
            zz = lax.rem(at.z + step, SIDE)
            if n >= 2:
                core_copy(s, n - 2, zz).wait_send()
            gradient_tile(s, zz * 2 + 1 - at.core, xs.at[n % 2])
            core_copy(s, n, zz).start()
            if n:
                got = fetch_pair(s, n - 1)
            gradient_tile(s, zz * 2 + at.core, own.at[s, zz])
            if n:
                got.wait()
                pair_sum(s, n - 1)

        def grad(i, carry):
            put(i, dot(right[0, s], wu[s, pl.ds(pl.multiple_of(i * tile, tile), tile), :], 1, 1), xg.at[1, s])
            return carry

        lax.fori_loop(0, d_tiles, grad, 0)
        fetch_pair(s, 3).wait()
        pair_sum(s, 3)
        for n in (2, 3):
            core_copy(s, n, 0).wait_send()

    def result_rows(t, s, h, other):
        block = st.at[0, h, s] if t == 0 else xg.at[1, s, h]
        return block.at[:, other] if h == 0 else block.at[other]

    def return1(t, s):
        copies = []
        for h in (0, 1):
            mine = at.second_at(h)
            dst = rec.at[t, h, :, s, mine]
            kept = pltpu.make_async_copy(result_rows(t, s, h, mine), dst, own_sem.at[t, s, h])
            kept.start()
            for k in steps:
                peer_at = lax.rem(mine + k, SIDE)
                copies.append(
                    send(result_rows(t, s, h, peer_at), dst, r1_s.at[t, s, h, k], r1_r.at[t, s, h, k], at.second(h, k))
                )
            copies.append(kept)
        return copies

    returning = {}
    for s in (0, 1):
        for c in moving[0, s]:
            c.wait_recv()
        forward(s)
        if s == 1:
            returning[0, 1] = return1(0, 1)
        for c in moving[1, s]:
            c.wait_recv()
        if s == 0:
            returning[0, 0] = return1(0, 0)
        backward(s)
        returning[1, s] = return1(1, s)

    def arrived(copies):
        for c in copies:
            if c.is_remote:
                c.wait_recv()
            else:
                c.wait()

    last = {0: [], 1: []}

    def return2(t):
        items = [(h, k) for h in (0, 1) for k in (1, 2, 3, 0)]

        def fetch(n):
            h, k = items[n]
            copy = pltpu.make_async_copy(
                rec.at[t, h, lax.rem(at.first_at(h) + k, SIDE)], rbuf.at[n % 2], rb_sem.at[n % 2]
            )
            copy.start()
            return copy

        ahead = fetch(0)
        for n, (h, k) in enumerate(items):
            ahead.wait()
            if n + 1 < len(items):
                ahead = fetch(n + 1)
            j = lax.rem(at.first_at(h) + k, SIDE)
            got = dot(pick[h, j], rbuf[n % 2].reshape(2 * SIDE * cap, half_w), 0, 0)
            p1[t, h, k] = got.astype(BF)
            if k:
                last[t].append(
                    send(p1.at[t, h, k], part.at[t, h, k - 1], r2_s.at[t, h, k], r2_r.at[t, h, k], at.first(h, k))
                )

    def finish(t):
        result = (out, ig)[t]
        for c in last[t]:
            c.wait_recv()
        for h in (0, 1):
            total = p1[t, h, 0].astype(F32)
            for k in steps:
                total = total + part[t, h, k - 1].astype(F32)
            result[:, h * half_w : (h + 1) * half_w] = total.astype(BF)

    def gradients(s):
        total = own[s, at.z].astype(F32)
        for k in steps:
            z_moving[s][(2, 1, 3).index(k)].wait_recv()
            copy = pltpu.make_async_copy(zr.at[s, k - 1], ld.at[k % 2], ld_sem.at[k % 2])
            copy.start()
            copy.wait()
            total = total + ld[k % 2].astype(F32)
        xs[s] = total.astype(BF)
        copy = pltpu.make_async_copy(xs.at[s], (g0_hbm, g1_hbm)[s], g_sem.at[s])
        copy.start()
        return copy

    arrived(returning[0, 0])
    arrived(returning[0, 1])
    return2(0)
    written = [gradients(0)]
    arrived(returning[1, 0])
    arrived(returning[1, 1])
    return2(1)
    finish(0)
    finish(1)
    written.append(gradients(1))
    for c in written:
        c.wait()
    for c in arriving[0] + arriving[1] + moving[1, 0] + moving[1, 1]:
        c.wait_send()
    for copies in list(returning.values()) + list(last.values()) + list(z_moving.values()):
        for c in copies:
            if c.is_remote:
                c.wait_send()


def body(tokens, expert_ids, combine_weight, partner, w_up, w_down, out_grad):
    toks, chosen = expert_ids.shape
    width = tokens.shape[1]
    half_w = width // 2
    hidden = w_up.shape[2]
    owners = SIDE * SIDE
    cap = toks * chosen * 4 // (3 * 2 * owners)
    rows = owners * cap
    pad = jnp.zeros((8 - chosen, toks), F32)
    route = jnp.concatenate([expert_ids.T.astype(F32), pad, combine_weight.T, pad], axis=0)
    any_ = pl.BlockSpec(memory_space=pl.ANY)
    vmem = pl.BlockSpec(memory_space=pltpu.VMEM)
    n_rows = width // (2 * SIDE)
    output, input_grad, first_grad, second_grad, *_ = pl.pallas_call(
        functools.partial(kernel, cap, chosen, 1.0 / toks),
        out_shape=(
            jax.ShapeDtypeStruct((toks, width), BF),
            jax.ShapeDtypeStruct((toks, width), BF),
            jax.ShapeDtypeStruct((n_rows, 2 * hidden), BF),
            jax.ShapeDtypeStruct((n_rows, 2 * hidden), BF),
            jax.ShapeDtypeStruct((2, 2, SIDE, 2, SIDE, cap, half_w), BF),
            jax.ShapeDtypeStruct((2, SIDE, n_rows, 2 * hidden), BF),
            jax.ShapeDtypeStruct((2, SIDE - 1, n_rows, 2 * hidden), BF),
        ),
        in_specs=[vmem, vmem, vmem, any_, any_],
        out_specs=(vmem, vmem, any_, any_, any_, any_, any_),
        scratch_shapes=[
            pltpu.VMEM((owners, 16, toks), F32),
            pltpu.VMEM((owners, 2 * owners, toks), F32),
            pltpu.VMEM((owners, 2 * owners, toks), F32),
            pltpu.VMEM((2, SIDE, 2 * SIDE * cap, toks), BF),
            pltpu.VMEM((2, 2, SIDE, toks, half_w), BF),
            pltpu.VMEM((2, 2, 2, SIDE, SIDE, cap, half_w), BF),
            pltpu.VMEM((2, 2, 2, SIDE, SIDE, cap, half_w), BF),
            pltpu.VMEM((2, width, hidden), BF),
            pltpu.VMEM((2, width, hidden), BF),
            pltpu.VMEM((2, 128, 2, hidden), BF),
            pltpu.VMEM((2, rows, toks), F32),
            pltpu.VMEM((2, rows, hidden), F32),
            pltpu.VMEM((2, 2, rows, hidden), BF),
            pltpu.VMEM((2, 2, SIDE - 1, toks, half_w), BF),
            pltpu.VMEM((2, 2, SIDE, cap, half_w), BF),
            pltpu.VMEM((2, SIDE, n_rows, 2 * hidden), BF),
            pltpu.VMEM((2, n_rows, 2 * hidden), BF),
            pltpu.VMEM((2, n_rows, 2 * hidden), BF),
            DMA((2, 4)), DMA((2, 4)),
            DMA((2, 2, 4)), DMA((2, 2, 4)),
            DMA((2, 2, 2, 4)), DMA((2, 2, 2, 4)),
            DMA((2,)),
            DMA((2, 2, 2, 4)), DMA((2, 2, 2, 4)), DMA((2, 2, 2)),
            DMA((2, 2, 4)), DMA((2, 2, 4)), DMA((2,)),
            DMA((2, 4)), DMA((2, 4)), DMA((2, 4)), DMA((2, 4)), DMA((2,)), DMA((2,)),
        ],
        compiler_params=pltpu.CompilerParams(
            collective_id=0, has_side_effects=True, vmem_limit_bytes=62 << 20
        ),
    )(route, tokens, out_grad, w_up, w_down)

    spread = lax.all_to_all(
        first_grad.reshape(owners, n_rows // owners, 2 * hidden), "expert", split_axis=0, concat_axis=0, tiled=True
    )
    choose = (partner[:, None] == jnp.arange(owners, dtype=jnp.int32)[None, :]).astype(BF)
    ordered = lax.dot_general(
        choose, spread, (((1,), (0,)), ((), ())), preferred_element_type=F32
    ).astype(BF)
    moved = lax.all_to_all(ordered, "expert", split_axis=0, concat_axis=0, tiled=True).reshape(n_rows, 2 * hidden)
    grad_up = jnp.stack([moved[:, :hidden], second_grad[:, :hidden]], axis=1)
    grad_down = jnp.stack([moved[:, hidden:], second_grad[:, hidden:]], axis=1)
    return (output, input_grad, grad_up, grad_down)


def solution(mesh):
    return jax.shard_map(
        body,
        mesh=mesh,
        in_specs=(
            P(("dp", "expert"), None),
            P(("dp", "expert"), None),
            P(("dp", "expert"), None),
            P(),
            P(None, "expert", None),
            P(None, "expert", None),
            P(("dp", "expert"), None),
        ),
        out_specs=(
            P(("dp", "expert"), None),
            P(("dp", "expert"), None),
            P("dp", "expert", None),
            P("dp", "expert", None),
        ),
        check_vma=False,
    )
```

time: 288 us -> 209 us (0.73)
  waiting for transfers between devices: 43.4 us -> 12.4 us
  Pallas kernels: 179 us -> 163 us
  local copies, waits for them, and re-layouts: 22.3 us -> 6.4 us
  between operations: 14.1 us -> 0.7 us
    reduce_scatter x2 -> x0, waiting for transfers between devices: 42.7 us -> none  [body(): lax.psum_scatter(dw[s], 'dp', scatter_dimension=0, tiled=True)]
    pallas_call x2 -> x1, Pallas kernels: 179 us -> 163 us  [body(): pl.pallas_call(functools.partial(kernel, cap, chosen, 1.0 / toks), out_sh...]
    all_to_all x1, waiting for transfers between devices: 0.01 us -> 12.4 us  [body(): lax.all_to_all(ordered, 'expert', split_axis=0, concat_axis=0, tiled=True)]
    squeeze x1 -> x0, local copies, waits for them, and re-layouts: 10.2 us -> none  [body(): dw[s]]
    unnamed x12, local copies, waits for them, and re-layouts: 9.53 us -> 4.98 us
  transfers between devices with their start and end apart: 3 -> 1, of which waited for: 1 -> 1; matrix products, arithmetic and copies ran while one was open for 1% -> 0% of each run, Pallas kernels for 26% -> 0%
where the time goes in v2:
time: 209 us; the launch traced here: 207 us
  Pallas kernels  163 us (78%)
  blocking collectives  18 us (9%)
  waiting for transfers between devices  12.4 us (6%)
  local copies, waits for them, and re-layouts  6.4 us (3%)
  starting transfers between devices  3.75 us (2%)
  other arithmetic  2.12 us (1%)
    pallas_call x1, Pallas kernels, body(): pl.pallas_call(functools.partial(kernel, cap, chosen, 1.0 / toks), out_sh...  163 us
    all_to_all x1, blocking collectives, body(): lax.all_to_all(first_grad.reshape(owners, n_rows // owners, 2 * hidden),...  18 us
    all_to_all x1, waiting for transfers between devices, body(): lax.all_to_all(ordered, 'expert', split_axis=0, concat_axis=0, tiled=True)  12.4 us
    unnamed x12, local copies, waits for them, and re-layouts  4.98 us
  transfers between devices with their start and end apart: 1, of which 1 were waited for; matrix products, arithmetic and copies ran while one was open for 0% of the time, Pallas kernels for 0%

profile of v2, /device:TPU:0, one launch (start us, length us, event | category | flops | bytes accessed | tf_op | source)
XLA Modules:
  0.0 207.0 jit_solution(8975691626119495662)
XLA Ops:
  0.6 0.7 convert_bitcast_fusion
  1.3 1.3 pad_maximum_fusion.2.route
  2.6 0.0 copy-start.3
  2.6 162.9 %shard_map.102 = (bf16[128,2048]{1,0:T(8,128)(2,1)}, bf16[128,2048]{1,0:T(8,128)(2,1)}, bf16[256,1536]{1,0:T(8,128)(2,1)}, bf16[256,1536]{1,0:T(8,128)(2,1)}, bf...) custom-call(f32[16,128]{1,0:T(8,128)} %pad_maximum_fusion.2.route, ...), custom_call_target="tpu_custom_call" | custom-call | tf_op jit(solution)/shard_map/pallas_call | solution.py:465
  165.6 0.0 copy-start
  165.6 18.0 %all_to_all.10 = bf16[16,16,1536]{2,1,0:T(8,128)(2,1)S(1)} all-to-all(bf16[16,16,1536]{2,1,0:T(8,128)(2,1)} %bitcast.17), channel_id=1, replica_groups=mesh['dp'=8,'expert'=16] {'expert'}, dimensions={0} | all-to-all | bytes 1572864 | tf_op jit(solution)/shard_map/all_to_all | solution.py:510
  183.6 0.0 copy-done.3
  183.6 0.6 convolution_convert_fusion
  184.3 0.0 copy-start.2
  184.3 1.3 copy.16
  185.6 0.0 copy-start.1
  185.6 3.7 %all-to-all-start.1 = ((bf16[16,16,1536]{2,1,0:T(8,128)(2,1)}), bf16[16,16,1536]{2,1,0:T(8,128)(2,1)S(1)}, u32[]{:S(2)}, u32[]{:S(2)}) async-start(bf16[16,16,1536]{2,1,0:T(8,128)(2,1)} %copy.16), calls=%async_computation.1 | async-start | bytes 1572864 | tf_op jit(solution)/shard_map/all_to_all | solution.py:517
  189.4 0.0 copy-done
  189.4 0.1 slice_bitcast_fusion.2
  189.4 12.4 %all-to-all-done.1 = bf16[16,16,1536]{2,1,0:T(8,128)(2,1)S(1)} async-done(((bf16[16,16,1536]{2,1,0:T(8,128)(2,1)}), bf16[16,16,1536]{2,1,0:T(8,128)(2,1)S(1)}, u32[]{:S(2)}, u32[]{:S(2)}) %all-to-all-start.1) | async-done | bytes 786464 | tf_op jit(solution)/shard_map/all_to_all | solution.py:517
  201.8 0.1 slice_bitcast_fusion
  201.8 0.1 pad_maximum_fusion
  202.0 1.7 copy.17
  203.7 1.7 copy.18
  205.4 0.0 copy-done.2
  205.4 0.8 copy.23
  206.2 0.0 copy-done.1
  206.2 0.8 copy.24
  (1 shorter events, 0.0 us)
Async XLA Ops:
  2.6 181.0 %copy-start.3 = (s32[16]{0:T(128)S(1)}, s32[16]{0:T(128)}, u32[]{:S(2)}) copy-start(s32[16]{0:T(128)} %param.10) | copy-start | bytes 196
  165.6 23.8 %copy-start = (bf16[256,1536]{1,0:T(8,128)(2,1)S(1)}, bf16[256,1536]{1,0:T(8,128)(2,1)}, u32[]{:S(2)}) copy-start(bf16[256,1536]{1,0:T(8,128)(2,1)} %get-tuple-element.11) | copy-start | bytes 2359300
  184.3 21.1 %copy-start.2 = (bf16[128,2048]{1,0:T(8,128)(2,1)S(1)}, bf16[128,2048]{1,0:T(8,128)(2,1)}, u32[]{:S(2)}) copy-start(bf16[128,2048]{1,0:T(8,128)(2,1)} %get-tuple-element.30) | copy-start | bytes 1572868
  185.6 20.6 %copy-start.1 = (bf16[128,2048]{1,0:T(8,128)(2,1)S(1)}, bf16[128,2048]{1,0:T(8,128)(2,1)}, u32[]{:S(2)}) copy-start(bf16[128,2048]{1,0:T(8,128)(2,1)} %get-tuple-element.31) | copy-start | bytes 1572868
  185.6 16.2 %all-to-all-start.1 = ((bf16[16,16,1536]{2,1,0:T(8,128)(2,1)}), bf16[16,16,1536]{2,1,0:T(8,128)(2,1)S(1)}, u32[]{:S(2)}, u32[]{:S(2)}) async-start(bf16[16,16,1536]{2,1,0:T(8,128)(2,1)} %copy.16), calls=%async_computation.1 | async-start | bytes 1572864 | tf_op jit(solution)/shard_map/all_to_all | solution.py:517

commit v3 on v2

--- a/solution.py
+++ b/solution.py
@@ -71,11 +71,11 @@
 
 def kernel(
     cap, chosen, scale,
-    route, tok, og, wu_hbm, wd_hbm,
-    out, ig, g0_hbm, g1_hbm, rec, cr, zr,
-    rt, rank, wt, pick, p1, st, xg, wu, wd, wbuf, wcol, slope, right, part, rbuf, own, xs, ld,
+    partner, route, tok, og, wu_hbm, wd_hbm,
+    out, ig, moved, g1_hbm, rec, cr, zr, ra, re,
+    rt, rank, wt, pick, p1, st, xg, wu, wd, wbuf, wcol, slope, right, part, rbuf, own, xs, ld, fin, rb, rd,
     rt_s, rt_r, p1_s, p1_r, p2_s, p2_r, w_sem, r1_s, r1_r, own_sem, r2_s, r2_r, rb_sem,
-    c_s, c_r, z_s, z_r, ld_sem, g_sem,
+    c_s, c_r, z_s, z_r, ld_sem, g_sem, m_s, m_r, mo_sem,
 ):
     at = Place()
     x, y, me = at.x, at.y, at.me
@@ -237,8 +237,6 @@
         c.wait_recv()
     stage(1)
     moving[1, 0] = phase2(1, 0)
-    moving[0, 1] = phase2(0, 1)
-    moving[1, 1] = phase2(1, 1)
     weights(wd_hbm, wd, n_chunks // 2, n_chunks)
 
     tile = 256
@@ -360,18 +358,24 @@
         return copies
 
     returning = {}
-    for s in (0, 1):
-        for c in moving[0, s]:
-            c.wait_recv()
-        forward(s)
-        if s == 1:
-            returning[0, 1] = return1(0, 1)
-        for c in moving[1, s]:
-            c.wait_recv()
-        if s == 0:
-            returning[0, 0] = return1(0, 0)
-        backward(s)
-        returning[1, s] = return1(1, s)
+    for c in moving[0, 0]:
+        c.wait_recv()
+    moving[0, 1] = phase2(0, 1)
+    forward(0)
+    for c in moving[1, 0]:
+        c.wait_recv()
+    moving[1, 1] = phase2(1, 1)
+    returning[0, 0] = return1(0, 0)
+    backward(0)
+    returning[1, 0] = return1(1, 0)
+    for c in moving[0, 1]:
+        c.wait_recv()
+    forward(1)
+    returning[0, 1] = return1(0, 1)
+    for c in moving[1, 1]:
+        c.wait_recv()
+    backward(1)
+    returning[1, 1] = return1(1, 1)
 
     def arrived(copies):
         for c in copies:
@@ -382,8 +386,8 @@
 
     last = {0: [], 1: []}
 
-    def return2(t):
-        items = [(h, k) for h in (0, 1) for k in (1, 2, 3, 0)]
+    def return2(t, h):
+        items = [(h, k) for k in (2, 1, 3, 0)]
 
         def fetch(n):
             h, k = items[n]
@@ -424,26 +428,93 @@
             copy.start()
             copy.wait()
             total = total + ld[k % 2].astype(F32)
-        xs[s] = total.astype(BF)
-        copy = pltpu.make_async_copy(xs.at[s], (g0_hbm, g1_hbm)[s], g_sem.at[s])
-        copy.start()
-        return copy
-
+        return total.astype(BF)
+
+    def exchange(number, src_of, dst_of, along):
+        copies = []
+        for u in (0, 1):
+            use_x = along[u]
+            mine = x if use_x else y
+            kept = pltpu.make_async_copy(src_of(u, mine), dst_of(u, mine), mo_sem.at[number, u])
+            kept.start()
+            copies.append(kept)
+            for k in steps:
+                peer = at.along_x(k) if use_x else at.along_y(k)
+                copies.append(
+                    send(
+                        src_of(u, lax.rem(mine + k, SIDE)), dst_of(u, mine),
+                        m_s.at[number, u, k], m_r.at[number, u, k], peer,
+                    )
+                )
+        return copies
+
+    relocating = []
+
+    def spread1():
+        relocating.append(
+            exchange(
+                0, lambda u, o: fin.at[u, :, o] if u == 0 else fin.at[u, o], lambda u, m: ra.at[u, m], (True, False)
+            )
+        )
+
+    def spread2():
+        relocating.append(
+            exchange(
+                1,
+                lambda u, o: ra.at[u, :, o],
+                lambda u, m: rb.at[u, m] if u == 0 else rb.at[u, :, m],
+                (False, True),
+            )
+        )
+
+    def gather1():
+        for i in range(SIDE * SIDE):
+            for u in (0, 1):
+                rd[u, i // SIDE, i % SIDE] = rb[u, partner[i] // SIDE, lax.rem(partner[i], SIDE)]
+        relocating.append(
+            exchange(
+                2, lambda u, o: rd.at[u, o] if u == 0 else rd.at[u, :, o], lambda u, m: re.at[u, m], (False, True)
+            )
+        )
+
+    def gather2():
+        relocating.append(
+            exchange(
+                3,
+                lambda u, o: re.at[u, :, o],
+                lambda u, m: moved.at[u, :, m] if u == 0 else moved.at[u, m],
+                (True, False),
+            )
+        )
+
+    total = gradients(0)
+    for u in (0, 1):
+        fin[u] = total[:, u * hidden : (u + 1) * hidden].reshape(fin.shape[1:])
+    spread1()
     arrived(returning[0, 0])
     arrived(returning[0, 1])
-    return2(0)
-    written = [gradients(0)]
+    return2(0, 0)
+    arrived(relocating[0])
+    spread2()
+    return2(0, 1)
+    arrived(relocating[1])
+    gather1()
     arrived(returning[1, 0])
     arrived(returning[1, 1])
-    return2(1)
+    return2(1, 0)
+    arrived(relocating[2])
+    gather2()
+    return2(1, 1)
     finish(0)
+    xs[1] = gradients(1)
+    written = pltpu.make_async_copy(xs.at[1], g1_hbm, g_sem)
+    written.start()
     finish(1)
-    written.append(gradients(1))
-    for c in written:
-        c.wait()
+    arrived(relocating[3])
+    written.wait()
     for c in arriving[0] + arriving[1] + moving[1, 0] + moving[1, 1]:
         c.wait_send()
-    for copies in list(returning.values()) + list(last.values()) + list(z_moving.values()):
+    for copies in list(returning.values()) + list(last.values()) + list(z_moving.values()) + relocating:
         for c in copies:
             if c.is_remote:
                 c.wait_send()
@@ -462,19 +533,22 @@
     any_ = pl.BlockSpec(memory_space=pl.ANY)
     vmem = pl.BlockSpec(memory_space=pltpu.VMEM)
     n_rows = width // (2 * SIDE)
-    output, input_grad, first_grad, second_grad, *_ = pl.pallas_call(
+    piece = n_rows // owners
+    output, input_grad, moved, second_grad, *_ = pl.pallas_call(
         functools.partial(kernel, cap, chosen, 1.0 / toks),
         out_shape=(
             jax.ShapeDtypeStruct((toks, width), BF),
             jax.ShapeDtypeStruct((toks, width), BF),
-            jax.ShapeDtypeStruct((n_rows, 2 * hidden), BF),
+            jax.ShapeDtypeStruct((2, SIDE, SIDE, piece, hidden), BF),
             jax.ShapeDtypeStruct((n_rows, 2 * hidden), BF),
             jax.ShapeDtypeStruct((2, 2, SIDE, 2, SIDE, cap, half_w), BF),
             jax.ShapeDtypeStruct((2, SIDE, n_rows, 2 * hidden), BF),
             jax.ShapeDtypeStruct((2, SIDE - 1, n_rows, 2 * hidden), BF),
+            jax.ShapeDtypeStruct((2, SIDE, SIDE, piece, hidden), BF),
+            jax.ShapeDtypeStruct((2, SIDE, SIDE, piece, hidden), BF),
         ),
-        in_specs=[vmem, vmem, vmem, any_, any_],
-        out_specs=(vmem, vmem, any_, any_, any_, any_, any_),
+        in_specs=[pl.BlockSpec(memory_space=pltpu.SMEM), vmem, vmem, vmem, any_, any_],
+        out_specs=(vmem, vmem, any_, any_, any_, any_, any_, any_, any_),
         scratch_shapes=[
             pltpu.VMEM((owners, 16, toks), F32),
             pltpu.VMEM((owners, 2 * owners, toks), F32),
@@ -494,29 +568,26 @@
             pltpu.VMEM((2, SIDE, n_rows, 2 * hidden), BF),
             pltpu.VMEM((2, n_rows, 2 * hidden), BF),
             pltpu.VMEM((2, n_rows, 2 * hidden), BF),
+            pltpu.VMEM((2, SIDE, SIDE, piece, hidden), BF),
+            pltpu.VMEM((2, SIDE, SIDE, piece, hidden), BF),
+            pltpu.VMEM((2, SIDE, SIDE, piece, hidden), BF),
             DMA((2, 4)), DMA((2, 4)),
             DMA((2, 2, 4)), DMA((2, 2, 4)),
             DMA((2, 2, 2, 4)), DMA((2, 2, 2, 4)),
             DMA((2,)),
             DMA((2, 2, 2, 4)), DMA((2, 2, 2, 4)), DMA((2, 2, 2)),
             DMA((2, 2, 4)), DMA((2, 2, 4)), DMA((2,)),
-            DMA((2, 4)), DMA((2, 4)), DMA((2, 4)), DMA((2, 4)), DMA((2,)), DMA((2,)),
+            DMA((2, 4)), DMA((2, 4)), DMA((2, 4)), DMA((2, 4)), DMA((2,)), DMA,
+            DMA((4, 2, 4)), DMA((4, 2, 4)), DMA((4, 2)),
         ],
         compiler_params=pltpu.CompilerParams(
             collective_id=0, has_side_effects=True, vmem_limit_bytes=62 << 20
         ),
-    )(route, tokens, out_grad, w_up, w_down)
-
-    spread = lax.all_to_all(
-        first_grad.reshape(owners, n_rows // owners, 2 * hidden), "expert", split_axis=0, concat_axis=0, tiled=True
-    )
-    choose = (partner[:, None] == jnp.arange(owners, dtype=jnp.int32)[None, :]).astype(BF)
-    ordered = lax.dot_general(
-        choose, spread, (((1,), (0,)), ((), ())), preferred_element_type=F32
-    ).astype(BF)
-    moved = lax.all_to_all(ordered, "expert", split_axis=0, concat_axis=0, tiled=True).reshape(n_rows, 2 * hidden)
-    grad_up = jnp.stack([moved[:, :hidden], second_grad[:, :hidden]], axis=1)
-    grad_down = jnp.stack([moved[:, hidden:], second_grad[:, hidden:]], axis=1)
+    )(partner, route, tokens, out_grad, w_up, w_down)
+
+    moved = moved.reshape(2, n_rows, hidden)
+    grad_up = jnp.stack([moved[0], second_grad[:, :hidden]], axis=1)
+    grad_down = jnp.stack([moved[1], second_grad[:, hidden:]], axis=1)
     return (output, input_grad, grad_up, grad_down)
 
 

time: 209 us -> 193 us (0.923)
  the two profiles are of different devices: /device:TPU:0 before, /device:TPU:66 now
where the time goes in v3:
time: 193 us; the launch traced here: 191 us
  Pallas kernels  181 us (94%)
  local copies, waits for them, and re-layouts  7.39 us (4%)
  other arithmetic  2.12 us (1%)
    pallas_call x1, Pallas kernels, body(): pl.pallas_call(functools.partial(kernel, cap, chosen, 1.0 / toks), out_sh...  181 us
    unnamed x8, local copies, waits for them, and re-layouts  4.97 us

profile of v3, /device:TPU:66, one launch (start us, length us, event | category | flops | bytes accessed | tf_op | source)
XLA Modules:
  0.0 190.8 jit_solution(16877685863138485278)
XLA Ops:
  0.6 0.7 convert_bitcast_fusion
  1.3 1.3 pad_maximum_fusion.2.route
  2.6 180.6 %shard_map.102 = (bf16[128,2048]{1,0:T(8,128)(2,1)}, bf16[128,2048]{1,0:T(8,128)(2,1)}, bf16[2,4,4,16,768]{4,3,2,1,0:T(8,128)(2,1)}, bf16[256,1536]{1,0:T(8,128)...) custom-call(s32[16]{0:T(128)} %partner.1, ...), custom_call_target="tpu_custom_call" | custom-call | tf_op jit(solution)/shard_map/pallas_call | solution.py:537
  183.2 0.0 copy-start.1
  183.2 0.0 copy-start
  183.2 1.3 fusion
  184.5 1.2 slice_bitcast_fusion
  185.7 0.1 pad_maximum_fusion
  185.8 1.7 copy.11
  187.5 1.7 copy.12
  189.2 0.0 copy-done.1
  189.2 0.8 copy.15
  190.0 0.0 copy-done
  190.0 0.8 copy.16
  (1 shorter events, 0.0 us)
Async XLA Ops:
  183.2 6.0 %copy-start.1 = (bf16[128,2048]{1,0:T(8,128)(2,1)S(1)}, bf16[128,2048]{1,0:T(8,128)(2,1)}, u32[]{:S(2)}) copy-start(bf16[128,2048]{1,0:T(8,128)(2,1)} %get-tuple-element.26) | copy-start | bytes 1572868
  183.2 6.8 %copy-start = (bf16[128,2048]{1,0:T(8,128)(2,1)S(1)}, bf16[128,2048]{1,0:T(8,128)(2,1)}, u32[]{:S(2)}) copy-start(bf16[128,2048]{1,0:T(8,128)(2,1)} %get-tuple-element.27) | copy-start | bytes 1572868

commit v4 on v3

--- a/solution.py
+++ b/solution.py
@@ -72,10 +72,10 @@
 def kernel(
     cap, chosen, scale,
     partner, route, tok, og, wu_hbm, wd_hbm,
-    out, ig, moved, g1_hbm, rec, cr, zr, ra, re,
-    rt, rank, wt, pick, p1, st, xg, wu, wd, wbuf, wcol, slope, right, part, rbuf, own, xs, ld, fin, rb, rd,
-    rt_s, rt_r, p1_s, p1_r, p2_s, p2_r, w_sem, r1_s, r1_r, own_sem, r2_s, r2_r, rb_sem,
-    c_s, c_r, z_s, z_r, ld_sem, g_sem, m_s, m_r, mo_sem,
+    out, ig, moved_up, moved_down, kept_up, kept_down, zr, ra, re,
+    rt, rank, wt, pick, p1, st, xg, wu, wd, wbuf, wcol, slope, right, part, own, xs, ld, cr, fin, rb, rd,
+    rt_s, rt_r, p1_s, p1_r, p1_o, p2_s, p2_r, w_sem, r1_s, r1_r, own_sem, r2_s, r2_r,
+    c_s, c_r, z_s, z_r, ld_sem, g_sem, m_s, m_r, mo_sem, row_free, core_free,
 ):
     at = Place()
     x, y, me = at.x, at.y, at.me
@@ -88,36 +88,35 @@
 
     at.greet()
     rt[x * SIDE + y] = route[...]
-    sends = []
     first = [
         send(route, rt.at[x * SIDE + y], rt_s.at[0, k], rt_r.at[0, k], at.along_y(k)) for k in steps
     ]
 
+    def arrived(copies):
+        for c in copies:
+            if c.is_remote:
+                c.wait_recv()
+            else:
+                c.wait()
+
+    def sent(copies):
+        for c in copies:
+            if c.is_remote:
+                c.wait_send()
+
     def phase1(t):
-        src = (tok, og)[t]
-        out = []
+        copies = []
         for h in (0, 1):
+            block = (tok, og)[t].at[:, pl.ds(h * half_w, half_w)]
+            dst = p1.at[t, h, at.first_at(h)]
             for k in steps:
-                out.append(
-                    send(
-                        src.at[:, pl.ds(h * half_w, half_w)],
-                        p1.at[t, h, at.first_at(h)],
-                        p1_s.at[t, h, k], p1_r.at[t, h, k], at.first(h, k),
-                    )
-                )
-        return out
-
-    def own1(t):
-        src = (tok, og)[t]
-        for h in (0, 1):
-            p1[t, h, at.first_at(h)] = src[:, h * half_w : (h + 1) * half_w]
+                copies.append(send(block, dst, p1_s.at[t, h, k], p1_r.at[t, h, k], at.first(h, k)))
+            kept = pltpu.make_async_copy(block, dst, p1_o.at[t, h])
+            kept.start()
+            copies.append(kept)
+        return copies
 
     arriving = [phase1(0), None]
-    own1(0)
-    for c in first:
-        c.wait()
-    block = rt.at[pl.ds(x * SIDE, SIDE)]
-    second = [send(block, block, rt_s.at[1, k], rt_r.at[1, k], at.along_x(k)) for k in steps]
 
     def weights(hbm, vmem, lo, hi):
         def fetch(i):
@@ -141,7 +140,12 @@
 
         lax.fori_loop(lo, hi, turn, 0)
 
+    for c in first:
+        c.wait()
+    block = rt.at[pl.ds(x * SIDE, SIDE)]
+    second = [send(block, block, rt_s.at[1, k], rt_r.at[1, k], at.along_x(k)) for k in steps]
     n_chunks = wu.shape[1] // chunk
+    weights(wu_hbm, wu, 0, n_chunks // 4)
     for c in second:
         c.wait()
 
@@ -194,9 +198,7 @@
 
     lax.fori_loop(0, SIDE * SIDE, slot_weights, 0)
 
-    weights(wu_hbm, wu, 0, n_chunks // 4)
     arriving[1] = phase1(1)
-    own1(1)
     weights(wu_hbm, wu, n_chunks // 4, n_chunks)
 
     def stage(t):
@@ -228,13 +230,11 @@
         return out
 
     moving = {}
-    for c in arriving[0]:
-        c.wait_recv()
+    arrived(arriving[0])
     stage(0)
     moving[0, 0] = phase2(0, 0)
     weights(wd_hbm, wd, 0, n_chunks // 2)
-    for c in arriving[1]:
-        c.wait_recv()
+    arrived(arriving[1])
     stage(1)
     moving[1, 0] = phase2(1, 0)
     weights(wd_hbm, wd, n_chunks // 2, n_chunks)
@@ -262,8 +262,7 @@
             return carry
 
         lax.fori_loop(0, h_tiles, turn, 0)
-        for c in moving[0, s]:
-            c.wait_send()
+        sent(moving[0, s])
 
         def result(i, carry):
             put(i, dot(right[1, s], wd[s, pl.ds(pl.multiple_of(i * tile, tile), tile), :], 1, 1), st.at[0, :, s])
@@ -271,11 +270,16 @@
 
         lax.fori_loop(0, d_tiles, result, 0)
 
-    def core_copy(s, n, zz):
+    def core_copy(s, n):
         return pltpu.make_async_remote_copy(
-            src_ref=xs.at[n % 2], dst_ref=cr.at[s, zz], send_sem=c_s.at[s, n], recv_sem=c_r.at[s, n],
+            src_ref=xs.at[n % 2], dst_ref=cr.at[n], send_sem=c_s.at[s, n], recv_sem=c_r.at[s, n],
             device_id=at.other_core(), device_id_type=MESH,
         )
+
+    def release_rows(t, s):
+        for k in steps:
+            for peer in (at.along_x(k), at.along_y(k)):
+                pl.semaphore_signal(row_free.at[t, s], inc=1, device_id=peer, device_id_type=MESH)
 
     def gradient_tile(s, i, dst):
         cols = pl.ds(pl.multiple_of(lax.rem(i, per_half) * tile, tile), tile)
@@ -292,20 +296,14 @@
     z_moving = {0: [], 1: []}
 
     def pair_sum(s, n):
+        core_copy(s, n).wait_recv()
         step = quarters[n]
         zz = lax.rem(at.z + step, SIDE)
-        own[s, zz] = (own[s, zz].astype(F32) + ld[n % 2].astype(F32)).astype(BF)
+        own[s, zz] = (own[s, zz].astype(F32) + cr[n].astype(F32)).astype(BF)
         if step:
             z_moving[s].append(
                 send(own.at[s, zz], zr.at[s, step - 1], z_s.at[s, step], z_r.at[s, step], at.along_z(step))
             )
-
-    def fetch_pair(s, n):
-        zz = lax.rem(at.z + quarters[n], SIDE)
-        core_copy(s, n, zz).wait_recv()
-        copy = pltpu.make_async_copy(cr.at[s, zz], ld.at[n % 2], ld_sem.at[n % 2])
-        copy.start()
-        return copy
 
     def backward(s):
         def turn(n, carry):
@@ -315,38 +313,43 @@
             return carry
 
         lax.fori_loop(0, h_tiles, turn, 0)
+        if s:
+            pl.semaphore_wait(core_free, 1)
         for n, step in enumerate(quarters):
             zz = lax.rem(at.z + step, SIDE)
             if n >= 2:
-                core_copy(s, n - 2, zz).wait_send()
+                core_copy(s, n - 2).wait_send()
             gradient_tile(s, zz * 2 + 1 - at.core, xs.at[n % 2])
-            core_copy(s, n, zz).start()
-            if n:
-                got = fetch_pair(s, n - 1)
+            core_copy(s, n).start()
             gradient_tile(s, zz * 2 + at.core, own.at[s, zz])
             if n:
-                got.wait()
                 pair_sum(s, n - 1)
+        release_rows(1, s)
 
         def grad(i, carry):
             put(i, dot(right[0, s], wu[s, pl.ds(pl.multiple_of(i * tile, tile), tile), :], 1, 1), xg.at[1, s])
             return carry
 
         lax.fori_loop(0, d_tiles, grad, 0)
-        fetch_pair(s, 3).wait()
         pair_sum(s, 3)
+        if s == 0:
+            pl.semaphore_signal(core_free, inc=1, device_id=at.other_core(), device_id_type=MESH)
         for n in (2, 3):
-            core_copy(s, n, 0).wait_send()
+            core_copy(s, n).wait_send()
 
     def result_rows(t, s, h, other):
         block = st.at[0, h, s] if t == 0 else xg.at[1, s, h]
         return block.at[:, other] if h == 0 else block.at[other]
 
+    def home(t, s, h):
+        return st.at[1, h, s] if t == 0 else xg.at[0, s, h]
+
     def return1(t, s):
+        pl.semaphore_wait(row_free.at[t, s], 6)
         copies = []
         for h in (0, 1):
             mine = at.second_at(h)
-            dst = rec.at[t, h, :, s, mine]
+            dst = home(t, s, h).at[mine]
             kept = pltpu.make_async_copy(result_rows(t, s, h, mine), dst, own_sem.at[t, s, h])
             kept.start()
             for k in steps:
@@ -358,52 +361,32 @@
         return copies
 
     returning = {}
-    for c in moving[0, 0]:
-        c.wait_recv()
+    arrived(moving[0, 0])
     moving[0, 1] = phase2(0, 1)
     forward(0)
-    for c in moving[1, 0]:
-        c.wait_recv()
+    arrived(moving[1, 0])
     moving[1, 1] = phase2(1, 1)
+    sent(moving[1, 0])
+    release_rows(0, 0)
+    backward(0)
     returning[0, 0] = return1(0, 0)
-    backward(0)
     returning[1, 0] = return1(1, 0)
-    for c in moving[0, 1]:
-        c.wait_recv()
+    arrived(moving[0, 1])
     forward(1)
+    arrived(moving[1, 1])
+    sent(moving[1, 1])
+    release_rows(0, 1)
     returning[0, 1] = return1(0, 1)
-    for c in moving[1, 1]:
-        c.wait_recv()
     backward(1)
     returning[1, 1] = return1(1, 1)
 
-    def arrived(copies):
-        for c in copies:
-            if c.is_remote:
-                c.wait_recv()
-            else:
-                c.wait()
-
     last = {0: [], 1: []}
 
     def return2(t, h):
-        items = [(h, k) for k in (2, 1, 3, 0)]
-
-        def fetch(n):
-            h, k = items[n]
-            copy = pltpu.make_async_copy(
-                rec.at[t, h, lax.rem(at.first_at(h) + k, SIDE)], rbuf.at[n % 2], rb_sem.at[n % 2]
-            )
-            copy.start()
-            return copy
-
-        ahead = fetch(0)
-        for n, (h, k) in enumerate(items):
-            ahead.wait()
-            if n + 1 < len(items):
-                ahead = fetch(n + 1)
+        for k in (2, 1, 3, 0):
             j = lax.rem(at.first_at(h) + k, SIDE)
-            got = dot(pick[h, j], rbuf[n % 2].reshape(2 * SIDE * cap, half_w), 0, 0)
+            came = [home(t, s, h)[:, j].reshape(SIDE * cap, half_w) for s in (0, 1)]
+            got = dot(pick[h, j], jnp.concatenate(came, axis=0), 0, 0)
             p1[t, h, k] = got.astype(BF)
             if k:
                 last[t].append(
@@ -420,15 +403,26 @@
                 total = total + part[t, h, k - 1].astype(F32)
             result[:, h * half_w : (h + 1) * half_w] = total.astype(BF)
 
-    def gradients(s):
-        total = own[s, at.z].astype(F32)
-        for k in steps:
+    def gradients(s, keep):
+        room = (ld.at[0], ld.at[1], xs.at[0])
+        copies = []
+        for k in (1, 3, 2):
             z_moving[s][(2, 1, 3).index(k)].wait_recv()
-            copy = pltpu.make_async_copy(zr.at[s, k - 1], ld.at[k % 2], ld_sem.at[k % 2])
+            copy = pltpu.make_async_copy(zr.at[s, k - 1], room[k - 1], ld_sem.at[k - 1])
             copy.start()
+            copies.append(copy)
+        for copy in copies:
             copy.wait()
-            total = total + ld[k % 2].astype(F32)
-        return total.astype(BF)
+
+        def turn(r, carry):
+            some = pl.ds(pl.multiple_of(r * 16, 16), 16)
+            total = own[s, at.z, some].astype(F32)
+            for buf in room:
+                total = total + buf[some].astype(F32)
+            keep(r, total.astype(BF))
+            return carry
+
+        lax.fori_loop(0, xs.shape[1] // 16, turn, 0)
 
     def exchange(number, src_of, dst_of, along):
         copies = []
@@ -482,14 +476,19 @@
             exchange(
                 3,
                 lambda u, o: re.at[u, :, o],
-                lambda u, m: moved.at[u, :, m] if u == 0 else moved.at[u, m],
+                lambda u, m: moved_up.at[:, m] if u == 0 else moved_down.at[m],
                 (True, False),
             )
         )
 
-    total = gradients(0)
-    for u in (0, 1):
-        fin[u] = total[:, u * hidden : (u + 1) * hidden].reshape(fin.shape[1:])
+    def keep_first(r, total):
+        for u in (0, 1):
+            fin[u, r // SIDE, lax.rem(r, SIDE)] = total[:, u * hidden : (u + 1) * hidden]
+
+    def keep_second(r, total):
+        xs[1, pl.ds(pl.multiple_of(r * 16, 16), 16)] = total
+
+    gradients(0, keep_first)
     spread1()
     arrived(returning[0, 0])
     arrived(returning[0, 1])
@@ -506,18 +505,19 @@
     gather2()
     return2(1, 1)
     finish(0)
-    xs[1] = gradients(1)
-    written = pltpu.make_async_copy(xs.at[1], g1_hbm, g_sem)
-    written.start()
+    gradients(1, keep_second)
+    written = []
+    for u, dst in enumerate((kept_up, kept_down)):
+        copy = pltpu.make_async_copy(xs.at[1, :, pl.ds(u * hidden, hidden)], dst, g_sem.at[u])
+        copy.start()
+        written.append(copy)
     finish(1)
     arrived(relocating[3])
-    written.wait()
-    for c in arriving[0] + arriving[1] + moving[1, 0] + moving[1, 1]:
-        c.wait_send()
+    for c in written:
+        c.wait()
+    sent(arriving[0] + arriving[1])
     for copies in list(returning.values()) + list(last.values()) + list(z_moving.values()) + relocating:
-        for c in copies:
-            if c.is_remote:
-                c.wait_send()
+        sent(copies)
 
 
 def body(tokens, expert_ids, combine_weight, partner, w_up, w_down, out_grad):
@@ -534,20 +534,22 @@
     vmem = pl.BlockSpec(memory_space=pltpu.VMEM)
     n_rows = width // (2 * SIDE)
     piece = n_rows // owners
-    output, input_grad, moved, second_grad, *_ = pl.pallas_call(
+    tile_shape = jax.ShapeDtypeStruct((n_rows, hidden), BF)
+    piece_shape = (SIDE, SIDE, piece, hidden)
+    output, input_grad, moved_up, moved_down, kept_up, kept_down, *_ = pl.pallas_call(
         functools.partial(kernel, cap, chosen, 1.0 / toks),
         out_shape=(
             jax.ShapeDtypeStruct((toks, width), BF),
             jax.ShapeDtypeStruct((toks, width), BF),
-            jax.ShapeDtypeStruct((2, SIDE, SIDE, piece, hidden), BF),
-            jax.ShapeDtypeStruct((n_rows, 2 * hidden), BF),
-            jax.ShapeDtypeStruct((2, 2, SIDE, 2, SIDE, cap, half_w), BF),
-            jax.ShapeDtypeStruct((2, SIDE, n_rows, 2 * hidden), BF),
+            jax.ShapeDtypeStruct(piece_shape, BF),
+            jax.ShapeDtypeStruct(piece_shape, BF),
+            tile_shape,
+            tile_shape,
             jax.ShapeDtypeStruct((2, SIDE - 1, n_rows, 2 * hidden), BF),
-            jax.ShapeDtypeStruct((2, SIDE, SIDE, piece, hidden), BF),
-            jax.ShapeDtypeStruct((2, SIDE, SIDE, piece, hidden), BF),
+            jax.ShapeDtypeStruct((2, *piece_shape), BF),
+            jax.ShapeDtypeStruct((2, *piece_shape), BF),
         ),
-        in_specs=[pl.BlockSpec(memory_space=pltpu.SMEM), vmem, vmem, vmem, any_, any_],
+        in_specs=[pl.BlockSpec(memory_space=pltpu.SMEM), vmem, any_, any_, any_, any_],
         out_specs=(vmem, vmem, any_, any_, any_, any_, any_, any_, any_),
         scratch_shapes=[
             pltpu.VMEM((owners, 16, toks), F32),
@@ -564,30 +566,30 @@
             pltpu.VMEM((2, rows, hidden), F32),
             pltpu.VMEM((2, 2, rows, hidden), BF),
             pltpu.VMEM((2, 2, SIDE - 1, toks, half_w), BF),
-            pltpu.VMEM((2, 2, SIDE, cap, half_w), BF),
             pltpu.VMEM((2, SIDE, n_rows, 2 * hidden), BF),
             pltpu.VMEM((2, n_rows, 2 * hidden), BF),
             pltpu.VMEM((2, n_rows, 2 * hidden), BF),
-            pltpu.VMEM((2, SIDE, SIDE, piece, hidden), BF),
-            pltpu.VMEM((2, SIDE, SIDE, piece, hidden), BF),
-            pltpu.VMEM((2, SIDE, SIDE, piece, hidden), BF),
+            pltpu.VMEM((SIDE, n_rows, 2 * hidden), BF),
+            pltpu.VMEM((2, *piece_shape), BF),
+            pltpu.VMEM((2, *piece_shape), BF),
+            pltpu.VMEM((2, *piece_shape), BF),
             DMA((2, 4)), DMA((2, 4)),
-            DMA((2, 2, 4)), DMA((2, 2, 4)),
+            DMA((2, 2, 4)), DMA((2, 2, 4)), DMA((2, 2)),
             DMA((2, 2, 2, 4)), DMA((2, 2, 2, 4)),
             DMA((2,)),
             DMA((2, 2, 2, 4)), DMA((2, 2, 2, 4)), DMA((2, 2, 2)),
-            DMA((2, 2, 4)), DMA((2, 2, 4)), DMA((2,)),
-            DMA((2, 4)), DMA((2, 4)), DMA((2, 4)), DMA((2, 4)), DMA((2,)), DMA,
+            DMA((2, 2, 4)), DMA((2, 2, 4)),
+            DMA((2, 4)), DMA((2, 4)), DMA((2, 4)), DMA((2, 4)), DMA((3,)), DMA((2,)),
             DMA((4, 2, 4)), DMA((4, 2, 4)), DMA((4, 2)),
+            pltpu.SemaphoreType.REGULAR((2, 2)), pltpu.SemaphoreType.REGULAR,
         ],
         compiler_params=pltpu.CompilerParams(
             collective_id=0, has_side_effects=True, vmem_limit_bytes=62 << 20
         ),
     )(partner, route, tokens, out_grad, w_up, w_down)
 
-    moved = moved.reshape(2, n_rows, hidden)
-    grad_up = jnp.stack([moved[0], second_grad[:, :hidden]], axis=1)
-    grad_down = jnp.stack([moved[1], second_grad[:, hidden:]], axis=1)
+    grad_up = jnp.stack([moved_up.reshape(n_rows, hidden), kept_up], axis=1)
+    grad_down = jnp.stack([moved_down.reshape(n_rows, hidden), kept_down], axis=1)
     return (output, input_grad, grad_up, grad_down)
 
 

time: 193 us -> 189 us (0.979)
  the two profiles are of different devices: /device:TPU:66 before, /device:TPU:98 now
where the time goes in v4:
time: 189 us
  Pallas kernels  178 us (94%)
  local copies, waits for them, and re-layouts  4.97 us (3%)
  other arithmetic  4.44 us (2%)
    pallas_call x1, Pallas kernels, body(): pl.pallas_call(functools.partial(kernel, cap, chosen, 1.0 / toks), out_sh...  178 us
    unnamed x8, local copies, waits for them, and re-layouts  4.97 us

profile of v4, /device:TPU:98, one launch (start us, length us, event | category | flops | bytes accessed | tf_op | source)
XLA Modules:
  0.0 188.6 jit_solution(5452023792966698191)
XLA Ops:
  0.6 0.7 convert_bitcast_fusion
  1.3 1.3 pad_maximum_fusion.2.route
  2.6 178.5 %shard_map.102 = (bf16[128,2048]{1,0:T(8,128)(2,1)}, bf16[128,2048]{1,0:T(8,128)(2,1)}, bf16[4,4,16,768]{3,2,1,0:T(8,128)(2,1)}, bf16[4,4,16,768]{3,2,1,0:T(8,12...) custom-call(s32[16]{0:T(128)} %partner.1, ...), custom_call_target="tpu_custom_call" | custom-call | tf_op jit(solution)/shard_map/pallas_call | solution.py:539
  181.1 0.0 copy-start.1
  181.1 0.0 copy-start
  181.1 1.3 pad_maximum_fusion
  182.4 1.7 copy.11
  184.1 1.2 pad_maximum_fusion.1
  185.3 1.7 copy.12
  187.0 0.0 copy-done.1
  187.0 0.8 copy.15
  187.8 0.0 copy-done
  187.8 0.8 copy.16
  (1 shorter events, 0.0 us)
Async XLA Ops:
  181.1 5.9 %copy-start.1 = (bf16[128,2048]{1,0:T(8,128)(2,1)S(1)}, bf16[128,2048]{1,0:T(8,128)(2,1)}, u32[]{:S(2)}) copy-start(bf16[128,2048]{1,0:T(8,128)(2,1)} %get-tuple-element.24) | copy-start | bytes 1572868
  181.1 6.7 %copy-start = (bf16[128,2048]{1,0:T(8,128)(2,1)S(1)}, bf16[128,2048]{1,0:T(8,128)(2,1)}, u32[]{:S(2)}) copy-start(bf16[128,2048]{1,0:T(8,128)(2,1)} %get-tuple-element.25) | copy-start | bytes 1572868

commit v5 on v4

--- a/solution.py
+++ b/solution.py
@@ -71,7 +71,7 @@
 
 def kernel(
     cap, chosen, scale,
-    partner, route, tok, og, wu_hbm, wd_hbm,
+    partner, ids, gate, tok, og, wu_hbm, wd_hbm,
     out, ig, moved_up, moved_down, kept_up, kept_down, zr, ra, re,
     rt, rank, wt, pick, p1, st, xg, wu, wd, wbuf, wcol, slope, right, part, own, xs, ld, cr, fin, rb, rd,
     rt_s, rt_r, p1_s, p1_r, p1_o, p2_s, p2_r, w_sem, r1_s, r1_r, own_sem, r2_s, r2_r,
@@ -87,10 +87,10 @@
     steps = (1, 2, 3)
 
     at.greet()
-    rt[x * SIDE + y] = route[...]
-    first = [
-        send(route, rt.at[x * SIDE + y], rt_s.at[0, k], rt_r.at[0, k], at.along_y(k)) for k in steps
-    ]
+    route = rt.at[x * SIDE + y]
+    route[0:chosen] = ids[...].astype(F32)
+    route[8 : 8 + chosen] = gate[...]
+    first = [send(route, route, rt_s.at[0, k], rt_r.at[0, k], at.along_y(k)) for k in steps]
 
     def arrived(copies):
         for c in copies:
@@ -109,14 +109,24 @@
         for h in (0, 1):
             block = (tok, og)[t].at[:, pl.ds(h * half_w, half_w)]
             dst = p1.at[t, h, at.first_at(h)]
-            for k in steps:
+            for k in (1, 3):
                 copies.append(send(block, dst, p1_s.at[t, h, k], p1_r.at[t, h, k], at.first(h, k)))
             kept = pltpu.make_async_copy(block, dst, p1_o.at[t, h])
             kept.start()
             copies.append(kept)
         return copies
 
-    arriving = [phase1(0), None]
+    def forward1(t):
+        copies = []
+        part_rows = toks // 2
+        for h in (0, 1):
+            for k, sem in ((1, 2), (3, 0)):
+                arriving[t][3 * h + k // 2].wait_recv()
+                origin = lax.rem(at.first_at(h) + SIDE - k, SIDE)
+                block = p1.at[t, h, origin, pl.ds((k // 2) * part_rows, part_rows)]
+                copies.append(send(block, block, p1_s.at[t, h, sem], p1_r.at[t, h, sem], at.first(h, k)))
+            arriving[t][3 * h + 2].wait()
+        return copies
 
     def weights(hbm, vmem, lo, hi):
         def fetch(i):
@@ -144,8 +154,11 @@
         c.wait()
     block = rt.at[pl.ds(x * SIDE, SIDE)]
     second = [send(block, block, rt_s.at[1, k], rt_r.at[1, k], at.along_x(k)) for k in steps]
+    arriving = [phase1(0)]
     n_chunks = wu.shape[1] // chunk
     weights(wu_hbm, wu, 0, n_chunks // 4)
+    arriving.append(phase1(1))
+    passing = [forward1(0)]
     for c in second:
         c.wait()
 
@@ -187,19 +200,7 @@
 
     lax.fori_loop(0, SIDE, picks, 0)
 
-    def slot_weights(n, carry):
-        for s in (0, 1):
-            q = rank[n, pl.ds(s * owners + me, 1), :]
-            w = wt[n, pl.ds(s * owners + me, 1), :]
-            col = jnp.sum(jnp.where(place == q, w, 0.0), axis=1, keepdims=True)
-            row = (lax.rem(n, SIDE) * SIDE + n // SIDE) * cap
-            wcol[s, pl.ds(pl.multiple_of(row, cap), cap), :] = jnp.broadcast_to(col, (cap, toks))
-        return carry
-
-    lax.fori_loop(0, SIDE * SIDE, slot_weights, 0)
-
-    arriving[1] = phase1(1)
-    weights(wu_hbm, wu, n_chunks // 4, n_chunks)
+    passing.append(forward1(1))
 
     def stage(t):
         for h in (0, 1):
@@ -230,14 +231,27 @@
         return out
 
     moving = {}
-    arrived(arriving[0])
+    arrived(passing[0])
     stage(0)
     moving[0, 0] = phase2(0, 0)
-    weights(wd_hbm, wd, 0, n_chunks // 2)
-    arrived(arriving[1])
+    arrived(passing[1])
     stage(1)
     moving[1, 0] = phase2(1, 0)
-    weights(wd_hbm, wd, n_chunks // 2, n_chunks)
+    sent(passing[0] + passing[1])
+
+    def slot_weights(n, carry):
+        for s in (0, 1):
+            q = rank[n, pl.ds(s * owners + me, 1), :]
+            w = wt[n, pl.ds(s * owners + me, 1), :]
+            col = jnp.sum(jnp.where(place == q, w, 0.0), axis=1, keepdims=True)
+            row = (lax.rem(n, SIDE) * SIDE + n // SIDE) * cap
+            wcol[s, pl.ds(pl.multiple_of(row, cap), cap), :] = jnp.broadcast_to(col, (cap, toks))
+        return carry
+
+    lax.fori_loop(0, SIDE * SIDE, slot_weights, 0)
+
+    weights(wu_hbm, wu, n_chunks // 4, n_chunks)
+    weights(wd_hbm, wd, 0, n_chunks)
 
     tile = 256
     h_tiles = hidden // tile
@@ -490,11 +504,11 @@
 
     gradients(0, keep_first)
     spread1()
+    arrived(relocating[0])
+    spread2()
     arrived(returning[0, 0])
     arrived(returning[0, 1])
     return2(0, 0)
-    arrived(relocating[0])
-    spread2()
     return2(0, 1)
     arrived(relocating[1])
     gather1()
@@ -528,8 +542,6 @@
     owners = SIDE * SIDE
     cap = toks * chosen * 4 // (3 * 2 * owners)
     rows = owners * cap
-    pad = jnp.zeros((8 - chosen, toks), F32)
-    route = jnp.concatenate([expert_ids.T.astype(F32), pad, combine_weight.T, pad], axis=0)
     any_ = pl.BlockSpec(memory_space=pl.ANY)
     vmem = pl.BlockSpec(memory_space=pltpu.VMEM)
     n_rows = width // (2 * SIDE)
@@ -549,7 +561,7 @@
             jax.ShapeDtypeStruct((2, *piece_shape), BF),
             jax.ShapeDtypeStruct((2, *piece_shape), BF),
         ),
-        in_specs=[pl.BlockSpec(memory_space=pltpu.SMEM), vmem, any_, any_, any_, any_],
+        in_specs=[pl.BlockSpec(memory_space=pltpu.SMEM), vmem, vmem, any_, any_, any_, any_],
         out_specs=(vmem, vmem, any_, any_, any_, any_, any_, any_, any_),
         scratch_shapes=[
             pltpu.VMEM((owners, 16, toks), F32),
@@ -586,7 +598,7 @@
         compiler_params=pltpu.CompilerParams(
             collective_id=0, has_side_effects=True, vmem_limit_bytes=62 << 20
         ),
-    )(partner, route, tokens, out_grad, w_up, w_down)
+    )(partner, expert_ids.T, combine_weight.T, tokens, out_grad, w_up, w_down)
 
     grad_up = jnp.stack([moved_up.reshape(n_rows, hidden), kept_up], axis=1)
     grad_down = jnp.stack([moved_down.reshape(n_rows, hidden), kept_down], axis=1)

time: 189 us -> 179 us (0.947)
  the two profiles are of different devices: /device:TPU:98 before, /device:TPU:0 now
where the time goes in v5:
time: 179 us; the launch traced here: 178 us
  Pallas kernels  170 us (95%)
  local copies, waits for them, and re-layouts  4.97 us (3%)
  other arithmetic  2.46 us (1%)
    pallas_call x1, Pallas kernels, body(): pl.pallas_call(functools.partial(kernel, cap, chosen, 1.0 / toks), out_sh...  170 us
    unnamed x8, local copies, waits for them, and re-layouts  4.97 us

profile of v5, /device:TPU:0, one launch (start us, length us, event | category | flops | bytes accessed | tf_op | source)
XLA Modules:
  0.0 178.4 jit_solution(12245840100931415279)
XLA Ops:
  0.6 170.3 %shard_map.102 = (bf16[128,2048]{1,0:T(8,128)(2,1)}, bf16[128,2048]{1,0:T(8,128)(2,1)}, bf16[4,4,16,768]{3,2,1,0:T(8,128)(2,1)}, bf16[4,4,16,768]{3,2,1,0:T(8,12...) custom-call(s32[16]{0:T(128)} %partner.1, ...), custom_call_target="tpu_custom_call" | custom-call | tf_op jit(solution)/shard_map/pallas_call | solution.py:551
  170.9 0.0 copy-start.1
  171.0 0.0 copy-start
  171.0 1.3 pad_maximum_fusion
  172.2 1.7 copy.11
  173.9 1.2 pad_maximum_fusion.1
  175.1 1.7 copy.12
  176.8 0.0 copy-done.1
  176.8 0.8 copy.15
  177.6 0.0 copy-done
  177.6 0.8 copy.16
Async XLA Ops:
  170.9 5.9 %copy-start.1 = (bf16[128,2048]{1,0:T(8,128)(2,1)S(1)}, bf16[128,2048]{1,0:T(8,128)(2,1)}, u32[]{:S(2)}) copy-start(bf16[128,2048]{1,0:T(8,128)(2,1)} %get-tuple-element.24) | copy-start | bytes 1572868
  171.0 6.7 %copy-start = (bf16[128,2048]{1,0:T(8,128)(2,1)S(1)}, bf16[128,2048]{1,0:T(8,128)(2,1)}, u32[]{:S(2)}) copy-start(bf16[128,2048]{1,0:T(8,128)(2,1)} %get-tuple-element.25) | copy-start | bytes 1572868

commit v6 on v5

--- a/solution.py
+++ b/solution.py
@@ -395,25 +395,43 @@
     returning[1, 1] = return1(1, 1)
 
     last = {0: [], 1: []}
-
-    def return2(t, h):
-        for k in (2, 1, 3, 0):
-            j = lax.rem(at.first_at(h) + k, SIDE)
-            came = [home(t, s, h)[:, j].reshape(SIDE * cap, half_w) for s in (0, 1)]
-            got = dot(pick[h, j], jnp.concatenate(came, axis=0), 0, 0)
-            p1[t, h, k] = got.astype(BF)
-            if k:
-                last[t].append(
+    homing = {0: [], 1: []}
+
+    def return2(t):
+        for h in (0, 1):
+            for k in (2, 1, 3, 0):
+                j = lax.rem(at.first_at(h) + k, SIDE)
+                came = [home(t, s, h)[:, j].reshape(SIDE * cap, half_w) for s in (0, 1)]
+                p1[t, h, k] = dot(pick[h, j], jnp.concatenate(came, axis=0), 0, 0).astype(BF)
+                if k == 2:
+                    for way, sem in ((1, 2), (3, 0)):
+                        some = pl.ds((way // 2) * (toks // 2), toks // 2)
+                        last[t].append(
+                            send(
+                                p1.at[t, h, 2, some], part.at[t, h, 1, some],
+                                r2_s.at[t, h, sem], r2_r.at[t, h, sem], at.first(h, way),
+                            )
+                        )
+
+    def return3(t):
+        for c in last[t]:
+            c.wait_recv()
+        for h in (0, 1):
+            for k in (1, 3):
+                some = slice((k // 2) * (toks // 2), (k // 2 + 1) * (toks // 2))
+                total = p1[t, h, k, some].astype(F32) + part[t, h, 1, some].astype(F32)
+                p1[t, h, k, some] = total.astype(BF)
+                homing[t].append(
                     send(p1.at[t, h, k], part.at[t, h, k - 1], r2_s.at[t, h, k], r2_r.at[t, h, k], at.first(h, k))
                 )
 
     def finish(t):
         result = (out, ig)[t]
-        for c in last[t]:
+        for c in homing[t]:
             c.wait_recv()
         for h in (0, 1):
             total = p1[t, h, 0].astype(F32)
-            for k in steps:
+            for k in (1, 3):
                 total = total + part[t, h, k - 1].astype(F32)
             result[:, h * half_w : (h + 1) * half_w] = total.astype(BF)
 
@@ -508,16 +526,16 @@
     spread2()
     arrived(returning[0, 0])
     arrived(returning[0, 1])
-    return2(0, 0)
-    return2(0, 1)
+    return2(0)
     arrived(relocating[1])
     gather1()
+    return3(0)
     arrived(returning[1, 0])
     arrived(returning[1, 1])
-    return2(1, 0)
+    return2(1)
     arrived(relocating[2])
     gather2()
-    return2(1, 1)
+    return3(1)
     finish(0)
     gradients(1, keep_second)
     written = []
@@ -530,7 +548,7 @@
     for c in written:
         c.wait()
     sent(arriving[0] + arriving[1])
-    for copies in list(returning.values()) + list(last.values()) + list(z_moving.values()) + relocating:
+    for copies in list(returning.values()) + list(last.values()) + list(homing.values()) + list(z_moving.values()) + relocating:
         sent(copies)
 
 

time: 179 us -> 172 us (0.961)
  Pallas kernels: 170 us -> 163 us
    pallas_call x1, Pallas kernels: 170 us -> 163 us  [body(): pl.pallas_call(functools.partial(kernel, cap, chosen, 1.0 / toks), out_sh...]
where the time goes in v6:
time: 172 us; the launch traced here: 171 us
  Pallas kernels  163 us (95%)
  local copies, waits for them, and re-layouts  4.97 us (3%)
  other arithmetic  2.46 us (1%)
    pallas_call x1, Pallas kernels, body(): pl.pallas_call(functools.partial(kernel, cap, chosen, 1.0 / toks), out_sh...  163 us
    unnamed x8, local copies, waits for them, and re-layouts  4.97 us

profile of v6, /device:TPU:0, one launch (start us, length us, event | category | flops | bytes accessed | tf_op | source)
XLA Modules:
  0.0 170.6 jit_solution(10217415527278327807)
XLA Ops:
  0.6 162.5 %shard_map.102 = (bf16[128,2048]{1,0:T(8,128)(2,1)}, bf16[128,2048]{1,0:T(8,128)(2,1)}, bf16[4,4,16,768]{3,2,1,0:T(8,128)(2,1)}, bf16[4,4,16,768]{3,2,1,0:T(8,12...) custom-call(s32[16]{0:T(128)} %partner.1, ...), custom_call_target="tpu_custom_call" | custom-call | tf_op jit(solution)/shard_map/pallas_call | solution.py:569
  163.1 0.0 copy-start.1
  163.2 0.0 copy-start
  163.2 1.3 pad_maximum_fusion
  164.4 1.7 copy.11
  166.1 1.2 pad_maximum_fusion.1
  167.3 1.7 copy.12
  169.0 0.0 copy-done.1
  169.0 0.8 copy.15
  169.8 0.0 copy-done
  169.8 0.8 copy.16
Async XLA Ops:
  163.1 5.9 %copy-start.1 = (bf16[128,2048]{1,0:T(8,128)(2,1)S(1)}, bf16[128,2048]{1,0:T(8,128)(2,1)}, u32[]{:S(2)}) copy-start(bf16[128,2048]{1,0:T(8,128)(2,1)} %get-tuple-element.24) | copy-start | bytes 1572868
  163.2 6.7 %copy-start = (bf16[128,2048]{1,0:T(8,128)(2,1)S(1)}, bf16[128,2048]{1,0:T(8,128)(2,1)}, u32[]{:S(2)}) copy-start(bf16[128,2048]{1,0:T(8,128)(2,1)} %get-tuple-element.25) | copy-start | bytes 1572868

commit v7 on v6

--- a/solution.py
+++ b/solution.py
@@ -150,11 +150,11 @@
 
         lax.fori_loop(lo, hi, turn, 0)
 
+    arriving = [phase1(0)]
     for c in first:
         c.wait()
     block = rt.at[pl.ds(x * SIDE, SIDE)]
     second = [send(block, block, rt_s.at[1, k], rt_r.at[1, k], at.along_x(k)) for k in steps]
-    arriving = [phase1(0)]
     n_chunks = wu.shape[1] // chunk
     weights(wu_hbm, wu, 0, n_chunks // 4)
     arriving.append(phase1(1))

time: 172 us -> 167 us (0.971)
  Pallas kernels: 163 us -> 159 us
    pallas_call x1, Pallas kernels: 163 us -> 159 us  [body(): pl.pallas_call(functools.partial(kernel, cap, chosen, 1.0 / toks), out_sh...]
where the time goes in v7:
time: 167 us
  Pallas kernels  159 us (95%)
  local copies, waits for them, and re-layouts  4.97 us (3%)
  other arithmetic  2.46 us (1%)
    pallas_call x1, Pallas kernels, body(): pl.pallas_call(functools.partial(kernel, cap, chosen, 1.0 / toks), out_sh...  159 us
    unnamed x8, local copies, waits for them, and re-layouts  4.97 us

profile of v7, /device:TPU:0, one launch (start us, length us, event | category | flops | bytes accessed | tf_op | source)
XLA Modules:
  0.0 166.8 jit_solution(5501168299921284090)
XLA Ops:
  0.6 158.7 %shard_map.102 = (bf16[128,2048]{1,0:T(8,128)(2,1)}, bf16[128,2048]{1,0:T(8,128)(2,1)}, bf16[4,4,16,768]{3,2,1,0:T(8,128)(2,1)}, bf16[4,4,16,768]{3,2,1,0:T(8,12...) custom-call(s32[16]{0:T(128)} %partner.1, ...), custom_call_target="tpu_custom_call" | custom-call | tf_op jit(solution)/shard_map/pallas_call | solution.py:569
  159.3 0.0 copy-start.1
  159.3 0.0 copy-start
  159.4 1.3 pad_maximum_fusion
  160.6 1.7 %copy.11 = bf16[256,2,768]{2,1,0:T(2,128)(2,1)} copy(bf16[256,2,768]{2,0,1:T(8,128)(2,1)S(1)} %pad_maximum_fusion) | data formatting | bytes 1572864
  162.3 1.2 pad_maximum_fusion.1
  163.5 1.7 %copy.12 = bf16[256,2,768]{2,1,0:T(2,128)(2,1)} copy(bf16[256,2,768]{2,0,1:T(8,128)(2,1)S(1)} %pad_maximum_fusion.1) | data formatting | bytes 1572864
  165.2 0.0 copy-done.1
  165.2 0.8 copy.15
  166.0 0.0 copy-done
  166.0 0.8 copy.16
Async XLA Ops:
  159.3 5.9 %copy-start.1 = (bf16[128,2048]{1,0:T(8,128)(2,1)S(1)}, bf16[128,2048]{1,0:T(8,128)(2,1)}, u32[]{:S(2)}) copy-start(bf16[128,2048]{1,0:T(8,128)(2,1)} %get-tuple-element.24) | copy-start | bytes 1572868
  159.3 6.7 %copy-start = (bf16[128,2048]{1,0:T(8,128)(2,1)S(1)}, bf16[128,2048]{1,0:T(8,128)(2,1)}, u32[]{:S(2)}) copy-start(bf16[128,2048]{1,0:T(8,128)(2,1)} %get-tuple-element.25) | copy-start | bytes 1572868
